TPU v7x, 32 devices: a whole 2x2x4 slice. The times are simulated.
32 devices in a mesh: dp: 4 (over x, core), sp: 8 (over z, y).
Axes of the slice: x: 2, y: 2, z: 4, core: 2. Of those that a mesh axis runs over, the one named last changes fastest.
Arguments:
- frames_in: bfloat16 [2048, 64, 256], P(('dp', 'sp')), may hold values from -6 to 6
- spatial_weight: bfloat16 [3, 3, 256, 256], replicated, may hold values from -0.125 to 0.125
- temporal_weight: bfloat16 [3, 256, 256], replicated, may hold values from -0.21875 to 0.21875
- cotangent: bfloat16 [2048, 64, 256], P(('dp', 'sp')), may hold values from -6 to 6
Outputs:
- block_out: bfloat16 [2048, 64, 256], P(('dp', 'sp'))
- grad_input: bfloat16 [2048, 64, 256], P(('dp', 'sp'))
- grad_spatial: float32 [3, 3, 256, 256], replicated
- grad_temporal: float32 [3, 256, 256], replicated
All inputs are finite; a program needn't handle non-finite values.
Results may differ from a plain program's by a relative error of at most 0.0049.
Values may be sent and summed in bfloat16 or wider, within the bound.
A program may use at most 128 MiB of HBM per device.

v0:
```python
import math

import jax
import jax.numpy as jnp
from jax import lax
from jax.sharding import PartitionSpec as P

H = 64
FRAMES = 4


def contract_rows(left, right):
    return lax.dot_general(
        left, right, (((0,), (0,)), ((), ())), preferred_element_type=jnp.float32
    )


def times_transpose(left, weight):
    return lax.dot_general(
        left, weight, (((1,), (1,)), ((), ())), preferred_element_type=jnp.float32
    )


def local(frames_in, spatial_weight, temporal_weight, cotangent):
    slab_rows, width_cells, channels = frames_in.shape
    sp_count = lax.axis_size("sp")

    def padded_rows(values):
        return jnp.pad(values, ((1, 1), (1, 1), (0, 0)))

    def flatten_rows(values):
        return values.reshape(-1, channels)

    padded_in = padded_rows(frames_in)
    pre = jnp.zeros((slab_rows * width_cells, channels), jnp.float32)
    for tap_row in range(3):
        for tap_col in range(3):
            window = flatten_rows(
                padded_in[tap_row : tap_row + slab_rows, tap_col : tap_col + width_cells]
            )
            pre = pre + jnp.dot(
                window, spatial_weight[tap_row, tap_col], preferred_element_type=jnp.float32
            )
    act = jax.nn.silu(pre).astype(jnp.bfloat16).reshape(slab_rows, width_cells, channels)

    def to_frames(values):
        return lax.all_to_all(values, "sp", split_axis=0, concat_axis=1, tiled=True)

    moved_act, moved_cot = (
        lax.all_to_all(act, "sp", split_axis=1, concat_axis=0, tiled=True),
        lax.all_to_all(cotangent, "sp", split_axis=1, concat_axis=0, tiled=True),
    )
    group_rows = slab_rows * sp_count
    stripe = width_cells // sp_count
    groups = group_rows // (FRAMES * H)
    act_clips = moved_act.reshape(groups, FRAMES, H * stripe, channels)
    cot_clips = moved_cot.reshape(groups, FRAMES, H * stripe, channels)
    act_padded = jnp.pad(act_clips, ((0, 0), (2, 0), (0, 0), (0, 0)))
    cot_padded = jnp.pad(cot_clips, ((0, 0), (0, 2), (0, 0), (0, 0)))
    temporal_sum = jnp.zeros(act_clips.shape, jnp.float32)
    act_grad_sum = jnp.zeros(act_clips.shape, jnp.float32)
    temporal_terms = []
    for tap_step in range(3):
        earlier = act_padded[:, 2 - tap_step : 2 - tap_step + FRAMES]
        temporal_sum = temporal_sum + jnp.einsum(
            "gfpc,cd->gfpd", earlier, temporal_weight[tap_step], preferred_element_type=jnp.float32
        )
        temporal_terms.append(
            jnp.einsum("gfpc,gfpd->cd", earlier, cot_clips, preferred_element_type=jnp.float32)
        )
        later = cot_padded[:, tap_step : tap_step + FRAMES]
        act_grad_sum = act_grad_sum + jnp.einsum(
            "gfpd,cd->gfpc", later, temporal_weight[tap_step], preferred_element_type=jnp.float32
        )
    temporal_out = to_frames(
        temporal_sum.astype(jnp.bfloat16).reshape(group_rows, stripe, channels)
    )
    grad_act = to_frames(act_grad_sum.astype(jnp.bfloat16).reshape(group_rows, stripe, channels))
    grad_temporal = jnp.stack(temporal_terms)
    grad_scale = 1.0 / math.sqrt(slab_rows * sp_count * lax.axis_size("dp") * width_cells)
    block_out = (frames_in.astype(jnp.float32) + temporal_out.astype(jnp.float32)).astype(
        jnp.bfloat16
    )
    sigma = jax.nn.sigmoid(pre)
    grad_pre = (
        flatten_rows(grad_act).astype(jnp.float32) * (sigma * (1.0 + pre * (1.0 - sigma)))
    ).astype(jnp.bfloat16)
    grad_padded = padded_rows(grad_pre.reshape(slab_rows, width_cells, channels))
    spatial_terms = []
    grad_in = flatten_rows(cotangent).astype(jnp.float32)
    for tap_row in range(3):
        for tap_col in range(3):
            window = flatten_rows(
                padded_in[tap_row : tap_row + slab_rows, tap_col : tap_col + width_cells]
            )
            spatial_terms.append(contract_rows(window, grad_pre))
            back_window = flatten_rows(
                grad_padded[
                    2 - tap_row : 2 - tap_row + slab_rows, 2 - tap_col : 2 - tap_col + width_cells
                ]
            )
            grad_in = grad_in + times_transpose(back_window, spatial_weight[tap_row, tap_col])
    grad_spatial = jnp.stack(spatial_terms).reshape(3, 3, channels, channels)
    grad_spatial, grad_temporal = lax.psum((grad_spatial, grad_temporal), ("dp", "sp"))
    grad_input = grad_in.astype(jnp.bfloat16).reshape(slab_rows, width_cells, channels)
    return (block_out, grad_input, grad_spatial * grad_scale, grad_temporal * grad_scale)


def solution(mesh):
    placed = (P(("dp", "sp"), None, None), P(), P(), P(("dp", "sp"), None, None))
    return jax.shard_map(
        local,
        mesh=mesh,
        in_specs=placed,
        out_specs=(P(("dp", "sp"), None, None), P(("dp", "sp"), None, None), P(), P()),
        check_vma=False,
    )
```

profile of v0, /device:TPU:0, one launch (start us, length us, event | category | flops | bytes accessed | tf_op | source)
XLA Modules:
  0.0 385.6 jit_solution(17746489602125472998)
XLA Ops:
  7.2 4.1 %copy.32 = bf16[64,64,256]{2,0,1:T(8,128)(2,1)} copy(bf16[64,64,256]{2,1,0:T(8,128)(2,1)} %param.7) | data formatting | bytes 4194304 | tf_op args[3]
  11.3 7.4 %all-to-all-start.2 = ((bf16[64,64,256]{2,0,1:T(8,128)(2,1)}), bf16[64,64,256]{2,0,1:T(8,128)(2,1)}, u32[]{:S(2)}, u32[]{:S(2)}) async-start(bf16[64,64,256]{2,0,1:T(8,128)(2,1)} %copy.32), calls=%async_computation.2 | async-start | bytes 4194304 | tf_op jit(solution)/shard_map/all_to_all | solution.py:51
  18.7 9.8 %pad_slice_fusion.10 = (bf16[64,64,256]{2,1,0:T(8,128)(2,1)}, bf16[64,64,256]{2,1,0:T(8,128)(2,1)}, bf16[64,64,256]{2,1,0:T(8,128)(2,1)}, bf16[64,64,256]{2,1,0:...) fusion(bf16[64,64,256]{2,1,0:T(8,128)(2,1)S(1)} %copy-done.3), kind=kLoop, calls=%fused_computation.46 | loop fusion | bytes 18874368 | tf_op jit(solution)/shard_map/slice | solution.py:39
  28.4 38.6 %all-to-all-done.2 = bf16[64,64,256]{2,0,1:T(8,128)(2,1)} async-done(((bf16[64,64,256]{2,0,1:T(8,128)(2,1)}), bf16[64,64,256]{2,0,1:T(8,128)(2,1)}, u32[]{:S(2)}, u32[]{:S(2)}) %all-to-all-start.2) | async-done | bytes 2097184 | tf_op jit(solution)/shard_map/all_to_all | solution.py:51
  67.0 2.9 copy.33
  71.4 2.1 add_convert_fusion
  73.5 5.0 %all-to-all-start.3 = ((bf16[512,8,256]{2,1,0:T(8,128)(2,1)}), bf16[512,8,256]{2,1,0:T(8,128)(2,1)}, u32[]{:S(2)}, u32[]{:S(2)}) async-start(bf16[512,8,256]{2,1,0:T(8,128)(2,1)} %bitcast.239), calls=%async_computation.3 | async-start | bytes 4194304 | tf_op jit(solution)/shard_map/all_to_all | solution.py:47
  78.5 2.4 fusion.63
  89.7 2.7 convolution_add_fusion.10
  92.4 34.0 %all-to-all-done.3 = bf16[512,8,256]{2,1,0:T(8,128)(2,1)} async-done(((bf16[512,8,256]{2,1,0:T(8,128)(2,1)}), bf16[512,8,256]{2,1,0:T(8,128)(2,1)}, u32[]{:S(2)}, u32[]{:S(2)}) %all-to-all-start.3) | async-done | bytes 2097184 | tf_op jit(solution)/shard_map/all_to_all | solution.py:47
  126.3 2.0 convert_bitcast_fusion
  128.9 1.6 copy-done.23
  131.2 3.5 fusion.2
  134.7 2.5 copy.29
  137.2 4.5 %all-to-all-start = ((bf16[64,64,256]{2,0,1:T(8,128)(2,1)}), bf16[64,64,256]{2,0,1:T(8,128)(2,1)}, u32[]{:S(2)}, u32[]{:S(2)}) async-start(bf16[64,64,256]{2,0,1:T(8,128)(2,1)} %copy.29), calls=%async_computation | async-start | bytes 4194304 | tf_op jit(solution)/shard_map/all_to_all | solution.py:50
  141.8 3.1 fusion.35
  149.2 1.0 fusion.31
  156.3 1.4 copy-done.24
  157.7 10.5 %pad_slice_fusion.2 = (bf16[64,64,256]{2,1,0:T(8,128)(2,1)}, bf16[64,64,256]{2,1,0:T(8,128)(2,1)S(1)}, bf16[64,64,256]{2,1,0:T(8,128)(2,1)S(1)}, bf16[64,64,256]...) fusion(bf16[64,64,256]{2,1,0:T(8,128)(2,1)S(1)} %bitcast.256), kind=kLoop, calls=%fused_computation.38 | loop fusion | bytes 18874368 | tf_op jit(solution)/shard_map/slice | solution.py:98
  171.3 2.8 convolution_add_fusion.4
  174.1 15.5 %all-to-all-done = bf16[64,64,256]{2,0,1:T(8,128)(2,1)} async-done(((bf16[64,64,256]{2,0,1:T(8,128)(2,1)}), bf16[64,64,256]{2,0,1:T(8,128)(2,1)}, u32[]{:S(2)}, u32[]{:S(2)}) %all-to-all-start) | async-done | bytes 2097184 | tf_op jit(solution)/shard_map/all_to_all | solution.py:50
  189.5 3.0 copy.30
  195.0 2.0 add_convert_fusion.1
  197.0 4.4 %all-to-all-start.1 = ((bf16[512,8,256]{2,1,0:T(8,128)(2,1)}), bf16[512,8,256]{2,1,0:T(8,128)(2,1)}, u32[]{:S(2)}, u32[]{:S(2)}) async-start(bf16[512,8,256]{2,1,0:T(8,128)(2,1)} %bitcast.238), calls=%async_computation.1 | async-start | bytes 4194304 | tf_op jit(solution)/shard_map/all_to_all | solution.py:47
  202.0 1.3 copy-done.2
  204.7 0.9 pad_maximum_fusion
  205.7 3.7 convolution_add_fusion.3
  212.6 2.1 fusion
  214.7 154.7 %all-reduce.7.cloned.1.call-done = (f32[3,3,256,256]{3,2,1,0:T(8,128)}, f32[3,256,256]{2,1,0:T(8,128)}) async-done(((f32[3,3,256,256]{3,2,1,0:T(8,128)}, f32[3,256,256]{2,1,0:T(8,128)}), (f32[3,3,256,256]{3,2,1,0:T(8,128)}, f32[3,256,256]{2,1,0:T(8,128)})) %all-reduce.7.cloned.1.call-update) | async-done | bytes 3145744 | tf_op jit(solution)/shard_map/psum | solution.py:104
  369.4 2.1 broadcast_multiply_fusion.1
  371.4 3.4 broadcast_multiply_fusion
  374.9 3.6 fusion.1
  (86 shorter events, 32.4 us)
Async XLA Ops:
  11.2 7.4 %copy-start.3 = (bf16[64,64,256]{2,1,0:T(8,128)(2,1)S(1)}, bf16[64,64,256]{2,1,0:T(8,128)(2,1)}, u32[]{:S(2)}) copy-start(bf16[64,64,256]{2,1,0:T(8,128)(2,1)} %param.4) | copy-start | bytes 6291460
  11.3 55.8 %all-to-all-start.2 = ((bf16[64,64,256]{2,0,1:T(8,128)(2,1)}), bf16[64,64,256]{2,0,1:T(8,128)(2,1)}, u32[]{:S(2)}, u32[]{:S(2)}) async-start(bf16[64,64,256]{2,0,1:T(8,128)(2,1)} %copy.32), calls=%async_computation.2 | async-start | bytes 4194304 | tf_op jit(solution)/shard_map/all_to_all | solution.py:51
  67.0 2.9 copy-start.27
  69.9 1.5 copy-start
  73.5 5.0 %copy-start.22 = (bf16[3,3,256,256]{3,2,1,0:T(8,128)(2,1)S(1)}, bf16[3,3,256,256]{3,2,1,0:T(8,128)(2,1)}, u32[]{:S(2)}) copy-start(bf16[3,3,256,256]{3,2,1,0:T(8,128)(2,1)} %param.5) | copy-start | bytes 3538948
  73.5 52.8 %all-to-all-start.3 = ((bf16[512,8,256]{2,1,0:T(8,128)(2,1)}), bf16[512,8,256]{2,1,0:T(8,128)(2,1)}, u32[]{:S(2)}, u32[]{:S(2)}) async-start(bf16[512,8,256]{2,1,0:T(8,128)(2,1)} %bitcast.239), calls=%async_computation.3 | async-start | bytes 4194304 | tf_op jit(solution)/shard_map/all_to_all | solution.py:47
  78.5 2.5 copy-start.19
  81.0 1.6 copy-start.16
  82.6 1.6 copy-start.13
  84.9 1.6 copy-start.10
  86.5 1.6 copy-start.8
  88.1 1.6 copy-start.6
  128.3 2.2 copy-start.23
  128.3 2.9 copy-start.25
  137.2 52.3 %all-to-all-start = ((bf16[64,64,256]{2,0,1:T(8,128)(2,1)}), bf16[64,64,256]{2,0,1:T(8,128)(2,1)}, u32[]{:S(2)}, u32[]{:S(2)}) async-start(bf16[64,64,256]{2,0,1:T(8,128)(2,1)} %copy.29), calls=%async_computation | async-start | bytes 4194304 | tf_op jit(solution)/shard_map/all_to_all | solution.py:50
  141.7 3.1 copy-start.20
  141.7 3.5 copy-start.21
  145.2 1.6 copy-start.17
  146.8 1.6 copy-start.14
  149.2 1.6 copy-start.11
  150.8 1.6 copy-start.9
  152.4 1.6 copy-start.7
  154.0 1.6 copy-start.26
  157.7 10.5 %copy-start.5 = (bf16[64,64,256]{2,1,0:T(8,128)(2,1)S(1)}, bf16[64,64,256]{2,1,0:T(8,128)(2,1)}, u32[]{:S(2)}) copy-start(bf16[64,64,256]{2,1,0:T(8,128)(2,1)} %param.7) | copy-start | bytes 6291460
  189.5 3.0 copy-start.1
  197.0 177.9 %all-to-all-start.1 = ((bf16[512,8,256]{2,1,0:T(8,128)(2,1)}), bf16[512,8,256]{2,1,0:T(8,128)(2,1)}, u32[]{:S(2)}, u32[]{:S(2)}) async-start(bf16[512,8,256]{2,1,0:T(8,128)(2,1)} %bitcast.238), calls=%async_computation.1 | async-start | bytes 4194304 | tf_op jit(solution)/shard_map/all_to_all | solution.py:47
  201.4 168.0 %all-reduce.7.cloned.1.call-start = ((), (), s32[]{:S(2)}) async-start(), calls=%async_computation.4 | async-start | bytes 6291456 | tf_op jit(solution)/shard_map/psum | solution.py:104
  201.7 1.6 copy-start.2
  205.7 3.7 copy-start.18
  209.4 1.6 copy-start.15
  211.0 1.6 copy-start.12
  371.4 3.4 copy-start.4
  (2 other events, 2.4 us)
Sparse Core Ops, SparseCore 0:
  208.4 160.9 all-reduce.6
where the time goes:
time: 393 us; the launch traced here: 386 us
  waiting for transfers between devices  243 us (62%)
  local copies, waits for them, and re-layouts  49.8 us (13%)
  matrix products  44.8 us (11%)
  starting transfers between devices  21.6 us (5%)
  between operations  14.7 us (4%)
  other arithmetic  12 us (3%)
    psum x1, waiting for transfers between devices, local(): lax.psum((grad_spatial, grad_temporal), ('dp', 'sp'))  155 us
    all_to_all x1, waiting for transfers between devices, local(): lax.all_to_all(cotangent, 'sp', split_axis=1, concat_axis=0, tiled=True)  38.6 us
    all_to_all x2, waiting for transfers between devices, to_frames(): return lax.all_to_all(values, 'sp', split_axis=0, concat_axis=1, tiled=True)  34 us
    unnamed x59, local copies, waits for them, and re-layouts  20.2 us
    all_to_all x1, waiting for transfers between devices, local(): lax.all_to_all(act, 'sp', split_axis=1, concat_axis=0, tiled=True)  15.5 us
    dot_general x9, matrix products, times_transpose(): lax.dot_general(left, weight, (((1,), (1,)), ((), ())), preferred_element...  13.2 us
    dot_general x9, matrix products, local(): jnp.dot(window, spatial_weight[tap_row, tap_col], preferred_element_type=...  12.9 us
    slice x1, local copies, waits for them, and re-layouts, local(): grad_padded[2 - tap_row:2 - tap_row + slab_rows, 2 - tap_col:2 - tap_col...  10.5 us
  transfers between devices with their start and end apart: 5, of which 4 were waited for; matrix products, arithmetic and copies ran while one was open for 16% of the time, Pallas kernels for 0%

commit v1 on v0

v1 whole, which is shorter than its diff:
```python
import functools
import math

import jax
import jax.numpy as jnp
from jax import lax
from jax.experimental import pallas as pl
from jax.experimental.pallas import tpu as pltpu
from jax.sharding import PartitionSpec as P

FRAMES = 4
BLOCKS = 4
VMEM_LIMIT = 50 * 1024 * 1024
MESH = pl.DeviceIdType.MESH
F32 = jnp.float32
BF16 = jnp.bfloat16


def store_shifted(dest, offset, values, width):
    cells, channels = values.shape
    column = lax.broadcasted_iota(jnp.int32, (cells, channels), 0) % width
    before = jnp.where(column == 0, 0.0, pltpu.roll(values, 1, axis=0))
    after = jnp.where(column == width - 1, 0.0, pltpu.roll(values, cells - 1, axis=0))
    dest[pl.ds(offset, cells), 0:channels] = before.astype(BF16)
    dest[pl.ds(offset, cells), channels : 2 * channels] = values.astype(BF16)
    dest[pl.ds(offset, cells), 2 * channels : 3 * channels] = after.astype(BF16)


def zero_edges(dest, width):
    rows, lanes = dest.shape
    dest[0:width] = jnp.zeros((width, lanes), BF16)
    dest[rows - width : rows] = jnp.zeros((width, lanes), BF16)


def forward_kernel(width, x_ref, w_ref, act_ref, slope_ref, x3):
    step = pl.program_id(0)
    cells, channels = act_ref.shape

    @pl.when(step == 0)
    def _():
        zero_edges(x3, width)
        for block in range(BLOCKS):
            store_shifted(
                x3,
                width + block * cells,
                x_ref[block * cells : (block + 1) * cells].astype(F32),
                width,
            )

    base = pl.multiple_of(step * cells, cells)
    pre = jnp.zeros((cells, channels), F32)
    for tap in range(3):
        pre = pre + jnp.dot(
            x3[pl.ds(base + tap * width, cells), :], w_ref[tap], preferred_element_type=F32
        )
    sigma = jax.nn.sigmoid(pre)
    act_ref[...] = (pre * sigma).astype(BF16)
    slope_ref[...] = (sigma * (1.0 + pre * (1.0 - sigma))).astype(BF16)


def backward_kernel(
    width, x_ref, cot_ref, cot1_ref, cot2_ref, act_ref, slope_ref, wt_ref, wf_ref,
    grad_in_ref, grads_ref, g3, temporal, spatial,
):
    step = pl.program_id(0)
    cells, channels = act_ref.shape

    @pl.when(step == 0)
    def _():
        zero_edges(g3, width)
        temporal[...] = jnp.zeros_like(temporal)
        spatial[...] = jnp.zeros_like(spatial)

    @pl.when(step < BLOCKS)
    def _():
        act_t = act_ref[...].T
        grad_act = jnp.zeros((cells, channels), F32)
        for tap, ref in enumerate((cot_ref, cot1_ref, cot2_ref)):
            grad_act = grad_act + jnp.dot(ref[...], wt_ref[tap], preferred_element_type=F32)
            temporal[tap] += jnp.dot(act_t, ref[...], preferred_element_type=F32)
        grad_pre = grad_act * slope_ref[...].astype(F32)
        store_shifted(g3, pl.multiple_of(width + step * cells, width), grad_pre, width)

    @pl.when(step >= BLOCKS)
    def _():
        base = pl.multiple_of((step - BLOCKS) * cells, cells)
        x_t = x_ref[...].T
        grad_in = cot_ref[...].astype(F32)
        for tap in range(3):
            window = g3[pl.ds(base + tap * width, cells), :]
            grad_in = grad_in + jnp.dot(window, wf_ref[tap], preferred_element_type=F32)
            spatial[tap] += jnp.dot(x_t, window, preferred_element_type=F32)
        grad_in_ref[...] = grad_in.astype(BF16)

    @pl.when(step == 2 * BLOCKS - 1)
    def _():
        for tap_row in range(3):
            for tap_col in range(3):
                place = (2 - tap_row) * 3 + 2 - tap_col
                grads_ref[place * channels : (place + 1) * channels] = spatial[
                    tap_row, :, tap_col * channels : (tap_col + 1) * channels
                ]
        for tap in range(3):
            grads_ref[(9 + tap) * channels : (10 + tap) * channels] = temporal[tap]


def temporal_kernel(x_ref, act_ref, act1_ref, act2_ref, w_ref, out_ref):
    total = jnp.dot(act_ref[...], w_ref[0], preferred_element_type=F32)
    total = total + jnp.dot(act1_ref[...], w_ref[1], preferred_element_type=F32)
    total = total + jnp.dot(act2_ref[...], w_ref[2], preferred_element_type=F32)
    total = total.astype(BF16).astype(F32)
    out_ref[...] = (x_ref[...].astype(F32) + total).astype(BF16)


def reduce_kernel(bits, grads_ref, full_ref, total, *scratch):
    levels = len(bits)
    sends, recvs = scratch[:levels], scratch[levels : 2 * levels]
    send_sem, recv_sem, back_send, back_recv = scratch[2 * levels :]
    here = {name: lax.axis_index(name) for name in ("dp", "sp")}

    def partner(level):
        name, bit = bits[level]
        mine = (here[name] // (1 << bit)) % 2
        other = here[name] + (1 - 2 * mine) * (1 << bit)
        ids = dict(here)
        ids[name] = other
        return mine, (ids["dp"], ids["sp"])

    partners = [partner(level) for level in range(levels)]
    barrier = pltpu.get_barrier_semaphore()
    for _, device in partners:
        pl.semaphore_signal(barrier, inc=1, device_id=device, device_id_type=MESH)
    pl.semaphore_wait(barrier, levels)

    rows = grads_ref.shape[0]
    half = grads_ref.shape[1] // 2

    def exchange(level):
        copy = pltpu.make_async_remote_copy(
            src_ref=sends[level],
            dst_ref=recvs[level],
            send_sem=send_sem.at[level],
            recv_sem=recv_sem.at[level],
            device_id=partners[level][1],
            device_id_type=MESH,
        )
        copy.start()
        return copy

    mine, _ = partners[0]
    keep = pl.multiple_of(mine * half, half)
    give = pl.multiple_of((1 - mine) * half, half)
    sends[0][...] = grads_ref[:, pl.ds(give, half)].astype(BF16)
    copy = exchange(0)
    copy.wait()
    total[...] = grads_ref[:, pl.ds(keep, half)] + recvs[0][...].astype(F32)
    start = 0
    size = rows
    starts = []
    for level in range(1, levels):
        size = size // 2
        mine, _ = partners[level]
        own = pl.multiple_of(start + mine * size, 16)
        other = pl.multiple_of(start + (1 - mine) * size, 16)
        sends[level][...] = total[pl.ds(other, size), :].astype(BF16)
        copy = exchange(level)
        copy.wait()
        total[pl.ds(own, size), :] += recvs[level][...].astype(F32)
        start = own
        starts.append(own)
    full_ref[pl.ds(start, size), pl.ds(keep, half)] = total[pl.ds(start, size), :].astype(BF16)
    for level in range(levels - 1, -1, -1):
        if level:
            own = pl.multiple_of(starts[level - 1], 16)
            place = full_ref.at[pl.ds(own, size), pl.ds(keep, half)]
        else:
            place = full_ref.at[:, pl.ds(keep, half)]
        copy = pltpu.make_async_remote_copy(
            src_ref=place,
            dst_ref=place,
            send_sem=back_send.at[level],
            recv_sem=back_recv.at[level],
            device_id=partners[level][1],
            device_id_type=MESH,
        )
        copy.start()
        copy.wait()
        size = size * 2


def reduce_all(grads):
    bits = []
    for name in ("dp", "sp"):
        count = lax.axis_size(name)
        bits += [(name, bit) for bit in range(count.bit_length() - 1)]
    rows, channels = grads.shape
    sizes = [rows >> level for level in range(len(bits))]
    pieces = [pltpu.VMEM((size, channels // 2), BF16) for size in sizes]
    semaphores = [pltpu.SemaphoreType.DMA((len(bits),))] * 4
    return pl.pallas_call(
        functools.partial(reduce_kernel, bits),
        out_shape=jax.ShapeDtypeStruct((rows, channels), BF16),
        in_specs=[pl.BlockSpec(memory_space=pltpu.VMEM)],
        out_specs=pl.BlockSpec(memory_space=pltpu.VMEM),
        scratch_shapes=[pltpu.VMEM((rows, channels // 2), F32)] + pieces + pieces + semaphores,
        compiler_params=pltpu.CompilerParams(
            collective_id=0, has_side_effects=True, vmem_limit_bytes=VMEM_LIMIT
        ),
        name="reduce_all",
    )(grads)


def whole(array):
    return pl.BlockSpec(array.shape, lambda step: (0,) * array.ndim)


def local(frames_in, spatial_weight, temporal_weight, cotangent):
    slab_rows, width, channels = frames_in.shape
    sp_count = lax.axis_size("sp")
    cells = slab_rows * width
    block = cells // BLOCKS
    x = frames_in.reshape(cells, channels)
    cot = cotangent.reshape(cells, channels)
    params = pltpu.CompilerParams(
        dimension_semantics=("arbitrary",), vmem_limit_bytes=VMEM_LIMIT
    )

    def shift(values, by):
        pairs = [
            (i, i + by)
            for i in range(sp_count)
            if 0 <= i + by < sp_count and (i + by) // FRAMES == i // FRAMES
        ]
        return lax.ppermute(values, "sp", pairs)

    cot1 = shift(cot, -1)
    cot2 = shift(cot, -2)

    w3 = spatial_weight.reshape(3, 3 * channels, channels)
    wf = spatial_weight[::-1, ::-1].transpose(0, 1, 3, 2).reshape(3, 3 * channels, channels)
    wt = temporal_weight.transpose(0, 2, 1)
    rows_spec = pl.BlockSpec((block, channels), lambda step: (step, 0))
    frame = jax.ShapeDtypeStruct((cells, channels), BF16)
    padded = pltpu.VMEM((cells + 2 * width, 3 * channels), BF16)

    act, slope = pl.pallas_call(
        functools.partial(forward_kernel, width),
        grid=(BLOCKS,),
        out_shape=(frame, frame),
        in_specs=[whole(x), whole(w3)],
        out_specs=(rows_spec, rows_spec),
        scratch_shapes=[padded],
        compiler_params=params,
        cost_estimate=pl.CostEstimate(
            flops=18 * cells * channels * channels,
            bytes_accessed=8 * cells * channels,
            transcendentals=2 * cells * channels,
        ),
        name="forward",
    )(x, w3)

    act1 = shift(act, 1)
    act2 = shift(act, 2)

    first = pl.BlockSpec((block, channels), lambda step: (jnp.minimum(step, BLOCKS - 1), 0))
    second = pl.BlockSpec((block, channels), lambda step: (jnp.maximum(step - BLOCKS, 0), 0))
    both = pl.BlockSpec((block, channels), lambda step: (step % BLOCKS, 0))
    grads_shape = jax.ShapeDtypeStruct((12 * channels, channels), F32)
    grad_in, grads = pl.pallas_call(
        functools.partial(backward_kernel, width),
        grid=(2 * BLOCKS,),
        out_shape=(frame, grads_shape),
        in_specs=[second, both, first, first, first, first, whole(wt), whole(wf)],
        out_specs=(second, whole(grads_shape)),
        scratch_shapes=[
            padded,
            pltpu.VMEM((3, channels, channels), F32),
            pltpu.VMEM((3, channels, 3 * channels), F32),
        ],
        compiler_params=params,
        cost_estimate=pl.CostEstimate(
            flops=48 * cells * channels * channels,
            bytes_accessed=18 * cells * channels,
            transcendentals=0,
        ),
        name="backward",
    )(x, cot, cot1, cot2, act, slope, wt, wf)

    reduced = reduce_all(grads)

    block_out = pl.pallas_call(
        temporal_kernel,
        grid=(BLOCKS,),
        out_shape=frame,
        in_specs=[rows_spec] * 4 + [whole(temporal_weight)],
        out_specs=rows_spec,
        compiler_params=params,
        cost_estimate=pl.CostEstimate(
            flops=6 * cells * channels * channels,
            bytes_accessed=10 * cells * channels,
            transcendentals=0,
        ),
        name="temporal",
    )(x, act, act1, act2, temporal_weight)

    grad_scale = 1.0 / math.sqrt(slab_rows * sp_count * lax.axis_size("dp") * width)
    scaled = reduced.astype(F32) * grad_scale
    grad_spatial = scaled[: 9 * channels].reshape(3, 3, channels, channels)
    grad_temporal = scaled[9 * channels :].reshape(3, channels, channels)
    return (
        block_out.reshape(frames_in.shape),
        grad_in.reshape(frames_in.shape),
        grad_spatial,
        grad_temporal,
    )


def solution(mesh):
    placed = (P(("dp", "sp"), None, None), P(), P(), P(("dp", "sp"), None, None))
    return jax.shard_map(
        local,
        mesh=mesh,
        in_specs=placed,
        out_specs=(P(("dp", "sp"), None, None), P(("dp", "sp"), None, None), P(), P()),
        check_vma=False,
    )
```

time: 393 us -> 179 us (0.46); the launches traced: 386 us -> 178 us
  waiting for transfers between devices: 243 us -> 18.8 us
  Pallas kernels: 0 us -> 131 us
  matrix products: 44.8 us -> 0 us
  local copies, waits for them, and re-layouts: 49.8 us -> 10.1 us
  between operations: 14.7 us -> 0.69 us
  other arithmetic: 12 us -> 0.28 us
  starting transfers between devices: 21.6 us -> 17.5 us
    psum x1 -> x0, waiting for transfers between devices: 155 us -> none  [local(): lax.psum((grad_spatial, grad_temporal), ('dp', 'sp'))]
    pallas_call x0 -> x4, Pallas kernels: none -> 131 us  [the longest x1 96.3 us: reduce_all(): pl.pallas_call(functools.partial(reduce_kernel, bits), out_shape=jax.Shap...]
    all_to_all x4 -> x0, waiting for transfers between devices: 88 us -> none  [the longest x1 38.6 us: local(): lax.all_to_all(cotangent, 'sp', split_axis=1, concat_axis=0, tiled=True)]
    dot_general x36 -> x0, matrix products: 44.8 us -> none  [the longest x9 13.2 us: times_transpose(): lax.dot_general(left, weight, (((1,), (1,)), ((), ())), preferred_element...]
    all_to_all x4 -> x0, starting transfers between devices: 21.3 us -> none  [the longest x2 9.36 us: to_frames(): return lax.all_to_all(values, 'sp', split_axis=0, concat_axis=1, tiled=True)]
    ppermute x0 -> x4, waiting for transfers between devices: none -> 18.8 us  [shift(): return lax.ppermute(values, 'sp', pairs)]
    slice x3 -> x2, local copies, waits for them, and re-layouts: 20.5 us -> 2.49 us  [the longest x1 1.56 us: local(): grad_spatial = scaled[:9 * channels].reshape(3, 3, channels, channels)]
    ppermute x0 -> x4, starting transfers between devices: none -> 17.5 us  [shift(): return lax.ppermute(values, 'sp', pairs)]
  transfers between devices with their start and end apart: 5 -> 4, of which waited for: 4 -> 2; matrix products, arithmetic and copies ran while one was open for 16% -> 4% of each run, Pallas kernels for 0% -> 70%
where the time goes in v1:
time: 179 us; the launch traced here: 178 us
  Pallas kernels  131 us (73%)
  waiting for transfers between devices  18.8 us (11%)
  starting transfers between devices  17.5 us (10%)
  local copies, waits for them, and re-layouts  10.1 us (6%)
    pallas_call x1, Pallas kernels, reduce_all(): pl.pallas_call(functools.partial(reduce_kernel, bits), out_shape=jax.Shap...  96.3 us
    pallas_call x1, Pallas kernels, local(): pl.pallas_call(functools.partial(backward_kernel, width), grid=(2 * BLOCK...  19.6 us
    ppermute x4, waiting for transfers between devices, shift(): return lax.ppermute(values, 'sp', pairs)  18.8 us
    ppermute x4, starting transfers between devices, shift(): return lax.ppermute(values, 'sp', pairs)  17.5 us
    pallas_call x1, Pallas kernels, local(): pl.pallas_call(functools.partial(forward_kernel, width), grid=(BLOCKS,),...  9.44 us
    pallas_call x1, Pallas kernels, local(): pl.pallas_call(temporal_kernel, grid=(BLOCKS,), out_shape=frame, in_specs...  5.65 us
    transpose x2, local copies, waits for them, and re-layouts, local(): spatial_weight[::-1, ::-1].transpose(0, 1, 3, 2)  4.88 us
  transfers between devices with their start and end apart: 4, of which 2 were waited for; matrix products, arithmetic and copies ran while one was open for 4% of the time, Pallas kernels for 70%

profile of v1, /device:TPU:0, one launch (start us, length us, event | category | flops | bytes accessed | tf_op | source)
XLA Modules:
  0.0 178.4 jit_solution(14978681269901084788)
XLA Ops:
  0.6 1.3 collective-permute-start.3
  1.9 1.3 collective-permute-start.2
  3.2 0.0 copy-start.2
  3.2 1.3 copy-done.2
  4.5 0.0 copy-start.1
  4.5 9.4 %forward.1 = (bf16[4096,256]{1,0:T(8,128)(2,1)}, bf16[4096,256]{1,0:T(8,128)(2,1)}) custom-call(bf16[4096,256]{1,0:T(8,128)(2,1)} %bitcast.11, bf16[3,768,256]{2,1,0:T(8,128)(2,1)S(1)} %bitcast.14), custom_call_target="tpu_custom_call" | custom-call | flops 4831838208 | bytes 8388608 | tf_op jit(solution)/shard_map/forward/pallas_call | solution.py:246
  13.9 8.4 %collective-permute-start.1 = (bf16[4096,256]{1,0:T(8,128)(2,1)}, bf16[4096,256]{1,0:T(8,128)(2,1)}, u32[]{:S(2)}, u32[]{:S(2)}) collective-permute-start(bf16[4096,256]{1,0:T(8,128)(2,1)} %get-tuple-element.8.act_ref), channel_id=1, source_target_pairs={{0,2},{1,3},{4,6},{5,7},{8,10},{9,11},{12,14},{13,15},{16,18},{17,... | collective-permute-start | bytes 6291464 | tf_op jit(solution)/shard_map/ppermute | solution.py:234
  22.3 6.6 %collective-permute-start = (bf16[4096,256]{1,0:T(8,128)(2,1)}, bf16[4096,256]{1,0:T(8,128)(2,1)}, u32[]{:S(2)}, u32[]{:S(2)}) collective-permute-start(bf16[4096,256]{1,0:T(8,128)(2,1)} %get-tuple-element.8.act_ref), channel_id=1, source_target_pairs={{0,1},{1,2},{2,3},{4,5},{5,6},{6,7},{8,9},{9,10},{10,11},{12,13},{... | collective-permute-start | bytes 6291464 | tf_op jit(solution)/shard_map/ppermute | solution.py:234
  28.9 0.0 copy-done.1
  28.9 0.2 copy.8
  29.0 0.0 copy-start
  29.1 2.5 %reverse_bitcast_fusion = bf16[3,3,256,256]{2,3,1,0:T(8,128)(2,1)} fusion(bf16[3,3,256,256]{3,2,1,0:T(8,128)(2,1)} %param.5), kind=kLoop, calls=%fused_computation.1 | loop fusion | bytes 2359296 | tf_op jit(solution)/shard_map/transpose | solution.py:240
  31.6 2.4 %copy.9 = bf16[3,3,256,256]{3,2,1,0:T(8,128)(2,1)} copy(bf16[3,3,256,256]{2,3,1,0:T(8,128)(2,1)} %reverse_bitcast_fusion) | data formatting | bytes 2359296 | tf_op jit(solution)/shard_map/transpose | solution.py:240
  33.9 17.8 %collective-permute-done.3.cot2_ref = bf16[4096,256]{1,0:T(8,128)(2,1)} collective-permute-done((bf16[4096,256]{1,0:T(8,128)(2,1)}, bf16[4096,256]{1,0:T(8,128)(2,1)}, u32[]{:S(2)}, u32[]{:S(2)}) %collective-permute-start.3) | collective-permute-done | bytes 2097184 | tf_op jit(solution)/shard_map/ppermute | solution.py:234
  51.7 1.0 collective-permute-done.2.cot1_ref
  52.7 0.0 copy-done
  52.7 0.0 copy-start.3
  52.8 1.3 copy-done.3
  54.0 19.6 %backward.1 = (bf16[4096,256]{1,0:T(8,128)(2,1)}, f32[3072,256]{1,0:T(8,128)}) custom-call(bf16[4096,256]{1,0:T(8,128)(2,1)S(1)} %bitcast.12, bf16[4096,256]{1,0:T(8,128)(2,1)} %bitcast.22, bf16[4096,256]{1,0:T(8,128)(2,1)} %collective-permute-done.2.cot1_ref, bf16[4096,256]{1,0:T(8,128)(2,1)} %collective-permute-done.3.cot2_ref, ...), custom_call_target="tpu_custom_call" | custom-call | flops 12884901888 | bytes 18874368 | tf_op jit(solution)/shard_map/backward/pallas_call | solution.py:269
  73.6 96.3 %reduce_all.1 = bf16[3072,256]{1,0:T(8,128)(2,1)S(1)} custom-call(f32[3072,256]{1,0:T(8,128)} %get-tuple-element.11.grads_ref), custom_call_target="tpu_custom_call" | custom-call | tf_op jit(solution)/shard_map/reduce_all/pallas_call | solution.py:200
  169.9 0.3 convert_multiply_fusion
  170.2 0.9 slice.9
  171.1 1.6 slice.8
  172.7 0.0 collective-permute-done.1.act2_ref
  172.7 0.0 collective-permute-done.act1_ref
  172.7 5.7 %temporal.1 = bf16[4096,256]{1,0:T(8,128)(2,1)} custom-call(bf16[4096,256]{1,0:T(8,128)(2,1)S(1)} %bitcast.13, bf16[4096,256]{1,0:T(8,128)(2,1)} %get-tuple-element.8.act_ref, bf16[4096,256]{1,0:T(8,128)(2,1)} %collective-permute-done.act1_ref, bf16[4096,256]{1,0:T(8,128)(2,1)} %collective-permute-done.1.act2_ref, bf16[3,256,256]{2,1,0:T(8,128)(2,1)S(1)} %copy-done.1), custom_call_target="tpu_custom_call" | custom-call | flops 1610612736 | bytes 10485760 | tf_op jit(solution)/shard_map/temporal/pallas_call | solution.py:291
Async XLA Ops:
  0.6 51.1 %collective-permute-start.3 = (bf16[4096,256]{1,0:T(8,128)(2,1)}, bf16[4096,256]{1,0:T(8,128)(2,1)}, u32[]{:S(2)}, u32[]{:S(2)}) collective-permute-start(bf16[4096,256]{1,0:T(8,128)(2,1)} %bitcast.20), channel_id=1, source_target_pairs={{2,0},{3,1},{6,4},{7,5},{10,8},{11,9},{14,12},{15,13},{18,16},{19,... | collective-permute-start | bytes 6291464 | tf_op jit(solution)/shard_map/ppermute | solution.py:234
  1.9 50.8 %collective-permute-start.2 = (bf16[4096,256]{1,0:T(8,128)(2,1)}, bf16[4096,256]{1,0:T(8,128)(2,1)}, u32[]{:S(2)}, u32[]{:S(2)}) collective-permute-start(bf16[4096,256]{1,0:T(8,128)(2,1)} %bitcast.21), channel_id=1, source_target_pairs={{1,0},{2,1},{3,2},{5,4},{6,5},{7,6},{9,8},{10,9},{11,10},{13,12},{... | collective-permute-start | bytes 6291464 | tf_op jit(solution)/shard_map/ppermute | solution.py:234
  3.2 1.3 copy-start.2
  4.5 24.4 %copy-start.1 = (bf16[3,256,256]{2,1,0:T(8,128)(2,1)S(1)}, bf16[3,256,256]{2,1,0:T(8,128)(2,1)}, u32[]{:S(2)}) copy-start(bf16[3,256,256]{2,1,0:T(8,128)(2,1)} %w_ref.1) | copy-start | bytes 1179652
  13.9 158.8 %collective-permute-start.1 = (bf16[4096,256]{1,0:T(8,128)(2,1)}, bf16[4096,256]{1,0:T(8,128)(2,1)}, u32[]{:S(2)}, u32[]{:S(2)}) collective-permute-start(bf16[4096,256]{1,0:T(8,128)(2,1)} %get-tuple-element.8.act_ref), channel_id=1, source_target_pairs={{0,2},{1,3},{4,6},{5,7},{8,10},{9,11},{12,14},{13,15},{16,18},{17,... | collective-permute-start | bytes 6291464 | tf_op jit(solution)/shard_map/ppermute | solution.py:234
  22.3 150.4 %collective-permute-start = (bf16[4096,256]{1,0:T(8,128)(2,1)}, bf16[4096,256]{1,0:T(8,128)(2,1)}, u32[]{:S(2)}, u32[]{:S(2)}) collective-permute-start(bf16[4096,256]{1,0:T(8,128)(2,1)} %get-tuple-element.8.act_ref), channel_id=1, source_target_pairs={{0,1},{1,2},{2,3},{4,5},{5,6},{6,7},{8,9},{9,10},{10,11},{12,13},{... | collective-permute-start | bytes 6291464 | tf_op jit(solution)/shard_map/ppermute | solution.py:234
  29.0 23.7 %copy-start = (bf16[64,64,256]{2,1,0:T(8,128)(2,1)S(1)}, bf16[64,64,256]{2,1,0:T(8,128)(2,1)}, u32[]{:S(2)}) copy-start(bf16[64,64,256]{2,1,0:T(8,128)(2,1)} %param.4) | copy-start | bytes 6291460
  52.7 1.3 copy-start.3

commit v2 on v1

--- a/solution.py
+++ b/solution.py
@@ -55,11 +55,11 @@
         )
     sigma = jax.nn.sigmoid(pre)
     act_ref[...] = (pre * sigma).astype(BF16)
-    slope_ref[...] = (sigma * (1.0 + pre * (1.0 - sigma))).astype(BF16)
+    slope_ref[...] = sigma * (1.0 + pre * (1.0 - sigma))
 
 
 def backward_kernel(
-    width, x_ref, cot_ref, cot1_ref, cot2_ref, act_ref, slope_ref, wt_ref, wf_ref,
+    width, x_ref, cot_ref, near_ref, far_lo_ref, far_hi_ref, via_lo_ref, via_hi_ref, act_ref, slope_ref, wt_ref, wf_ref,
     grad_in_ref, grads_ref, g3, temporal, spatial,
 ):
     step = pl.program_id(0)
@@ -75,10 +75,13 @@
     def _():
         act_t = act_ref[...].T
         grad_act = jnp.zeros((cells, channels), F32)
-        for tap, ref in enumerate((cot_ref, cot1_ref, cot2_ref)):
-            grad_act = grad_act + jnp.dot(ref[...], wt_ref[tap], preferred_element_type=F32)
-            temporal[tap] += jnp.dot(act_t, ref[...], preferred_element_type=F32)
-        grad_pre = grad_act * slope_ref[...].astype(F32)
+        low = step < BLOCKS // 2
+        next1 = near_ref[...] + jnp.where(low, via_lo_ref[...], via_hi_ref[...])
+        next2 = jnp.where(low, far_lo_ref[...], far_hi_ref[...])
+        for tap, later in enumerate((cot_ref[...], next1, next2)):
+            grad_act = grad_act + jnp.dot(later, wt_ref[tap], preferred_element_type=F32)
+            temporal[tap] += jnp.dot(act_t, later, preferred_element_type=F32)
+        grad_pre = grad_act * slope_ref[...]
         store_shifted(g3, pl.multiple_of(width + step * cells, width), grad_pre, width)
 
     @pl.when(step >= BLOCKS)
@@ -112,79 +115,90 @@
     out_ref[...] = (x_ref[...].astype(F32) + total).astype(BF16)
 
 
-def reduce_kernel(bits, grads_ref, full_ref, total, *scratch):
+def reduce_kernel(bits, chunks, grads_ref, full_ref, total, *scratch):
     levels = len(bits)
-    sends, recvs = scratch[:levels], scratch[levels : 2 * levels]
-    send_sem, recv_sem, back_send, back_recv = scratch[2 * levels :]
+    staged = scratch[:chunks]
+    recvs = scratch[chunks : chunks + chunks * levels]
+    send_sem, recv_sem, back_send, back_recv = scratch[chunks + chunks * levels :]
     here = {name: lax.axis_index(name) for name in ("dp", "sp")}
 
-    def partner(level):
-        name, bit = bits[level]
+    def partner(name, bit):
         mine = (here[name] // (1 << bit)) % 2
-        other = here[name] + (1 - 2 * mine) * (1 << bit)
         ids = dict(here)
-        ids[name] = other
+        ids[name] = here[name] + (1 - 2 * mine) * (1 << bit)
         return mine, (ids["dp"], ids["sp"])
 
-    partners = [partner(level) for level in range(levels)]
+    partners = [partner(name, bit) for name, bit in bits]
     barrier = pltpu.get_barrier_semaphore()
     for _, device in partners:
         pl.semaphore_signal(barrier, inc=1, device_id=device, device_id_type=MESH)
     pl.semaphore_wait(barrier, levels)
 
-    rows = grads_ref.shape[0]
+    rows = grads_ref.shape[0] // chunks
     half = grads_ref.shape[1] // 2
-
-    def exchange(level):
+    rest = partners[1:]
+    orders = []
+    for chunk in range(chunks):
+        turn = chunk % len(rest)
+        orders.append(partners[:1] + rest[turn:] + rest[:turn])
+
+    def send(chunk, level, source, dest, send_sems, recv_sems):
         copy = pltpu.make_async_remote_copy(
-            src_ref=sends[level],
-            dst_ref=recvs[level],
-            send_sem=send_sem.at[level],
-            recv_sem=recv_sem.at[level],
-            device_id=partners[level][1],
+            src_ref=source,
+            dst_ref=dest,
+            send_sem=send_sems.at[chunk * levels + level],
+            recv_sem=recv_sems.at[chunk * levels + level],
+            device_id=orders[chunk][level][1],
             device_id_type=MESH,
         )
         copy.start()
         return copy
 
-    mine, _ = partners[0]
+    mine = partners[0][0]
     keep = pl.multiple_of(mine * half, half)
     give = pl.multiple_of((1 - mine) * half, half)
-    sends[0][...] = grads_ref[:, pl.ds(give, half)].astype(BF16)
-    copy = exchange(0)
-    copy.wait()
-    total[...] = grads_ref[:, pl.ds(keep, half)] + recvs[0][...].astype(F32)
-    start = 0
+    copies = [
+        send(
+            chunk, 0, grads_ref.at[chunk * rows : (chunk + 1) * rows, pl.ds(give, half)],
+            recvs[chunk * levels], send_sem, recv_sem,
+        )
+        for chunk in range(chunks)
+    ]
+    for chunk in range(chunks):
+        copies[chunk].wait()
+        place = pl.ds(chunk * rows, rows)
+        total[place, :] = grads_ref[place, pl.ds(keep, half)] + recvs[chunk * levels][...]
+    starts = [[chunk * rows] for chunk in range(chunks)]
     size = rows
-    starts = []
     for level in range(1, levels):
         size = size // 2
-        mine, _ = partners[level]
-        own = pl.multiple_of(start + mine * size, 16)
-        other = pl.multiple_of(start + (1 - mine) * size, 16)
-        sends[level][...] = total[pl.ds(other, size), :].astype(BF16)
-        copy = exchange(level)
-        copy.wait()
-        total[pl.ds(own, size), :] += recvs[level][...].astype(F32)
-        start = own
-        starts.append(own)
-    full_ref[pl.ds(start, size), pl.ds(keep, half)] = total[pl.ds(start, size), :].astype(BF16)
+        copies = []
+        for chunk in range(chunks):
+            mine = orders[chunk][level][0]
+            start = starts[chunk][-1]
+            own = pl.multiple_of(start + mine * size, 16)
+            other = pl.multiple_of(start + (1 - mine) * size, 16)
+            source = total.at[pl.ds(other, size), :]
+            if level == 1:
+                staged[chunk][...] = total[pl.ds(other, size), :].astype(BF16)
+                source = staged[chunk]
+            dest = recvs[chunk * levels + level]
+            copies.append(send(chunk, level, source, dest, send_sem, recv_sem))
+            starts[chunk].append(own)
+        for chunk in range(chunks):
+            copies[chunk].wait()
+            arrived = recvs[chunk * levels + level][...].astype(F32)
+            total[pl.ds(starts[chunk][-1], size), :] += arrived
+    for chunk in range(chunks):
+        place = pl.ds(starts[chunk][-1], size)
+        full_ref[place, pl.ds(keep, half)] = total[place, :].astype(BF16)
     for level in range(levels - 1, -1, -1):
-        if level:
-            own = pl.multiple_of(starts[level - 1], 16)
-            place = full_ref.at[pl.ds(own, size), pl.ds(keep, half)]
-        else:
-            place = full_ref.at[:, pl.ds(keep, half)]
-        copy = pltpu.make_async_remote_copy(
-            src_ref=place,
-            dst_ref=place,
-            send_sem=back_send.at[level],
-            recv_sem=back_recv.at[level],
-            device_id=partners[level][1],
-            device_id_type=MESH,
-        )
-        copy.start()
-        copy.wait()
+        copies = []
+        for chunk in range(chunks):
+            place = full_ref.at[pl.ds(starts[chunk][level], size), pl.ds(keep, half)]
+            copies.append(send(chunk, level, place, place, back_send, back_recv))
+        for copy in copies:
+            copy.wait()
         size = size * 2
 
 
@@ -193,16 +207,24 @@
     for name in ("dp", "sp"):
         count = lax.axis_size(name)
         bits += [(name, bit) for bit in range(count.bit_length() - 1)]
-    rows, channels = grads.shape
-    sizes = [rows >> level for level in range(len(bits))]
-    pieces = [pltpu.VMEM((size, channels // 2), BF16) for size in sizes]
-    semaphores = [pltpu.SemaphoreType.DMA((len(bits),))] * 4
+    total_rows, channels = grads.shape
+    half = channels // 2
+    chunks = 3
+    rows = total_rows // chunks
+    levels = len(bits)
+    staged = [pltpu.VMEM((rows // 2, half), BF16)] * chunks
+    recvs = [
+        pltpu.VMEM((rows >> level, half), BF16 if level == 1 else F32)
+        for _ in range(chunks)
+        for level in range(levels)
+    ]
+    semaphores = [pltpu.SemaphoreType.DMA((chunks * levels,))] * 4
     return pl.pallas_call(
-        functools.partial(reduce_kernel, bits),
-        out_shape=jax.ShapeDtypeStruct((rows, channels), BF16),
+        functools.partial(reduce_kernel, bits, chunks),
+        out_shape=jax.ShapeDtypeStruct(grads.shape, BF16),
         in_specs=[pl.BlockSpec(memory_space=pltpu.VMEM)],
         out_specs=pl.BlockSpec(memory_space=pltpu.VMEM),
-        scratch_shapes=[pltpu.VMEM((rows, channels // 2), F32)] + pieces + pieces + semaphores,
+        scratch_shapes=[pltpu.VMEM((total_rows, half), F32)] + staged + recvs + semaphores,
         compiler_params=pltpu.CompilerParams(
             collective_id=0, has_side_effects=True, vmem_limit_bytes=VMEM_LIMIT
         ),
@@ -225,16 +247,18 @@
         dimension_semantics=("arbitrary",), vmem_limit_bytes=VMEM_LIMIT
     )
 
-    def shift(values, by):
+    def move(values, *steps):
         pairs = [
-            (i, i + by)
-            for i in range(sp_count)
-            if 0 <= i + by < sp_count and (i + by) // FRAMES == i // FRAMES
+            (clip + source, clip + target)
+            for clip in range(0, sp_count, FRAMES)
+            for source, target in steps
         ]
         return lax.ppermute(values, "sp", pairs)
 
-    cot1 = shift(cot, -1)
-    cot2 = shift(cot, -2)
+    middle = cells // 2
+    far_lo = move(cot[:middle], (2, 0), (3, 1))
+    near = move(cot, (1, 0), (3, 2))
+    far_hi = move(cot[middle:], (2, 0), (3, 1))
 
     w3 = spatial_weight.reshape(3, 3 * channels, channels)
     wf = spatial_weight[::-1, ::-1].transpose(0, 1, 3, 2).reshape(3, 3 * channels, channels)
@@ -246,7 +270,7 @@
     act, slope = pl.pallas_call(
         functools.partial(forward_kernel, width),
         grid=(BLOCKS,),
-        out_shape=(frame, frame),
+        out_shape=(frame, jax.ShapeDtypeStruct((cells, channels), F32)),
         in_specs=[whole(x), whole(w3)],
         out_specs=(rows_spec, rows_spec),
         scratch_shapes=[padded],
@@ -259,18 +283,28 @@
         name="forward",
     )(x, w3)
 
-    act1 = shift(act, 1)
-    act2 = shift(act, 2)
+    act2 = move(act, (0, 2), (1, 3))
+    far_lo, _ = lax.optimization_barrier((far_lo, act))
+    via_lo = move(far_lo, (0, 1))
+    far_hi, _ = lax.optimization_barrier((far_hi, act))
+    via_hi = move(far_hi, (0, 1))
+    act_late, via_lo, via_hi = lax.optimization_barrier((act, via_lo, via_hi))
+    act1 = move(act_late, (0, 1), (1, 2), (2, 3))
 
     first = pl.BlockSpec((block, channels), lambda step: (jnp.minimum(step, BLOCKS - 1), 0))
     second = pl.BlockSpec((block, channels), lambda step: (jnp.maximum(step - BLOCKS, 0), 0))
     both = pl.BlockSpec((block, channels), lambda step: (step % BLOCKS, 0))
+    lo = pl.BlockSpec((block, channels), lambda step: (jnp.minimum(step, BLOCKS // 2 - 1), 0))
+    hi = pl.BlockSpec(
+        (block, channels),
+        lambda step: (jnp.clip(step - BLOCKS // 2, 0, BLOCKS // 2 - 1), 0),
+    )
     grads_shape = jax.ShapeDtypeStruct((12 * channels, channels), F32)
     grad_in, grads = pl.pallas_call(
         functools.partial(backward_kernel, width),
         grid=(2 * BLOCKS,),
         out_shape=(frame, grads_shape),
-        in_specs=[second, both, first, first, first, first, whole(wt), whole(wf)],
+        in_specs=[second, both, first, lo, hi, lo, hi, first, first, whole(wt), whole(wf)],
         out_specs=(second, whole(grads_shape)),
         scratch_shapes=[
             padded,
@@ -284,7 +318,7 @@
             transcendentals=0,
         ),
         name="backward",
-    )(x, cot, cot1, cot2, act, slope, wt, wf)
+    )(x, cot, near, far_lo, far_hi, via_lo, via_hi, act, slope, wt, wf)
 
     reduced = reduce_all(grads)
 

time: 179 us -> 198 us (1.11)
  waiting for transfers between devices: 18.8 us -> 74.8 us
  Pallas kernels: 131 us -> 91.8 us
  starting transfers between devices: 17.5 us -> 19.8 us
    ppermute x4 -> x7, waiting for transfers between devices: 18.8 us -> 74.8 us  [move(): return lax.ppermute(values, 'sp', pairs)]
    pallas_call x1, Pallas kernels: 96.3 us -> 54.6 us  [reduce_all(): pl.pallas_call(functools.partial(reduce_kernel, bits, chunks), out_shape=...]
    pallas_call x1, Pallas kernels: 19.6 us -> 22.1 us  [local(): pl.pallas_call(functools.partial(backward_kernel, width), grid=(2 * BLOCK...]
    ppermute x4 -> x7, starting transfers between devices: 17.5 us -> 19.8 us  [move(): return lax.ppermute(values, 'sp', pairs)]
  transfers between devices with their start and end apart: 4 -> 7, of which waited for: 2 -> 4; matrix products, arithmetic and copies ran while one was open for 4% -> 4% of each run, Pallas kernels for 70% -> 44%
where the time goes in v2:
time: 198 us
  Pallas kernels  91.8 us (46%)
  waiting for transfers between devices  74.8 us (38%)
  starting transfers between devices  19.8 us (10%)
  local copies, waits for them, and re-layouts  10.2 us (5%)
    ppermute x7, waiting for transfers between devices, move(): return lax.ppermute(values, 'sp', pairs)  74.8 us
    pallas_call x1, Pallas kernels, reduce_all(): pl.pallas_call(functools.partial(reduce_kernel, bits, chunks), out_shape=...  54.6 us
    pallas_call x1, Pallas kernels, local(): pl.pallas_call(functools.partial(backward_kernel, width), grid=(2 * BLOCK...  22.1 us
    ppermute x7, starting transfers between devices, move(): return lax.ppermute(values, 'sp', pairs)  19.8 us
    pallas_call x1, Pallas kernels, local(): pl.pallas_call(functools.partial(forward_kernel, width), grid=(BLOCKS,),...  9.44 us
    pallas_call x1, Pallas kernels, local(): pl.pallas_call(temporal_kernel, grid=(BLOCKS,), out_shape=frame, in_specs...  5.65 us
    transpose x2, local copies, waits for them, and re-layouts, local(): spatial_weight[::-1, ::-1].transpose(0, 1, 3, 2)  4.73 us
  transfers between devices with their start and end apart: 7, of which 4 were waited for; matrix products, arithmetic and copies ran while one was open for 4% of the time, Pallas kernels for 44%

profile of v2, /device:TPU:0, one launch (start us, length us, event | category | flops | bytes accessed | tf_op | source)
XLA Modules:
  0.0 197.5 jit_solution(6200351987890783721)
XLA Ops:
  0.6 0.0 copy-start.3
  0.6 1.9 fusion
  2.5 1.3 collective-permute-start.2
  3.8 1.3 collective-permute-start
  5.1 1.3 collective-permute-start.6
  6.4 0.0 copy-done.3
  6.4 0.0 copy-start.2
  6.4 9.4 %forward.1 = (bf16[4096,256]{1,0:T(8,128)(2,1)S(1)}, f32[4096,256]{1,0:T(8,128)}) custom-call(bf16[4096,256]{1,0:T(8,128)(2,1)} %bitcast.13, bf16[3,768,256]{2,1,0:T(8,128)(2,1)S(1)} %bitcast.16), custom_call_target="tpu_custom_call" | custom-call | flops 4831838208 | bytes 8388608 | tf_op jit(solution)/shard_map/forward/pallas_call | solution.py:270
  15.9 0.0 copy-start.1
  15.9 15.0 %collective-permute-done.2.far_hi_ref = bf16[2048,256]{1,0:T(8,128)(2,1)} collective-permute-done((bf16[2048,256]{1,0:T(8,128)(2,1)S(1)}, bf16[2048,256]{1,0:T(8,128)(2,1)}, u32[]{:S(2)}, u32[]{:S(2)}) %collective-permute-start.2) | collective-permute-done | bytes 1048608 | tf_op jit(solution)/shard_map/ppermute | solution.py:256
  30.9 21.6 %collective-permute-done.far_lo_ref = bf16[2048,256]{1,0:T(8,128)(2,1)} collective-permute-done((bf16[2048,256]{1,0:T(8,128)(2,1)S(1)}, bf16[2048,256]{1,0:T(8,128)(2,1)}, u32[]{:S(2)}, u32[]{:S(2)}) %collective-permute-start) | collective-permute-done | bytes 1048608 | tf_op jit(solution)/shard_map/ppermute | solution.py:256
  52.6 5.2 %collective-permute-start.1 = (bf16[2048,256]{1,0:T(8,128)(2,1)}, bf16[2048,256]{1,0:T(8,128)(2,1)}, u32[]{:S(2)}, u32[]{:S(2)}) collective-permute-start(bf16[2048,256]{1,0:T(8,128)(2,1)} %collective-permute-done.far_lo_ref), channel_id=1, source_target_pairs={{0,1},{4,5},{8,9},{12,13},{16,17},{20,21},{24,25},{28,29}} | collective-permute-start | bytes 3145736 | tf_op jit(solution)/shard_map/ppermute | solution.py:256
  57.8 2.3 %collective-permute-start.3 = (bf16[2048,256]{1,0:T(8,128)(2,1)}, bf16[2048,256]{1,0:T(8,128)(2,1)}, u32[]{:S(2)}, u32[]{:S(2)}) collective-permute-start(bf16[2048,256]{1,0:T(8,128)(2,1)} %collective-permute-done.2.far_hi_ref), channel_id=1, source_target_pairs={{0,1},{4,5},{8,9},{12,13},{16,17},{20,21},{24,25},{28,29}} | collective-permute-start | bytes 3145736 | tf_op jit(solution)/shard_map/ppermute | solution.py:256
  60.0 2.7 %collective-permute-start.5 = (bf16[4096,256]{1,0:T(8,128)(2,1)S(1)}, bf16[4096,256]{1,0:T(8,128)(2,1)}, u32[]{:S(2)}, u32[]{:S(2)}) collective-permute-start(bf16[4096,256]{1,0:T(8,128)(2,1)S(1)} %get-tuple-element.16.act_ref), channel_id=1, source_target_pairs={{0,2},{1,3},{4,6},{5,7},{8,10},{9,11},{12,14},{13,15},{16,18},{17,... | collective-permute-start | bytes 6291464 | tf_op jit(solution)/shard_map/ppermute | solution.py:256
  62.8 0.0 copy-done.2
  62.8 0.2 copy.8
  62.9 17.7 %collective-permute-done.1.via_lo_ref = bf16[2048,256]{1,0:T(8,128)(2,1)} collective-permute-done((bf16[2048,256]{1,0:T(8,128)(2,1)}, bf16[2048,256]{1,0:T(8,128)(2,1)}, u32[]{:S(2)}, u32[]{:S(2)}) %collective-permute-start.1) | collective-permute-done | bytes 1048608 | tf_op jit(solution)/shard_map/ppermute | solution.py:256
  80.7 20.4 %collective-permute-done.3.via_hi_ref = bf16[2048,256]{1,0:T(8,128)(2,1)} collective-permute-done((bf16[2048,256]{1,0:T(8,128)(2,1)}, bf16[2048,256]{1,0:T(8,128)(2,1)}, u32[]{:S(2)}, u32[]{:S(2)}) %collective-permute-start.3) | collective-permute-done | bytes 1048608 | tf_op jit(solution)/shard_map/ppermute | solution.py:256
  101.1 5.7 %collective-permute-start.4 = (bf16[4096,256]{1,0:T(8,128)(2,1)S(1)}, bf16[4096,256]{1,0:T(8,128)(2,1)}, u32[]{:S(2)}, u32[]{:S(2)}) collective-permute-start(bf16[4096,256]{1,0:T(8,128)(2,1)S(1)} %get-tuple-element.16.act_ref), channel_id=1, source_target_pairs={{0,1},{1,2},{2,3},{4,5},{5,6},{6,7},{8,9},{9,10},{10,11},{12,13},{... | collective-permute-start | bytes 6291464 | tf_op jit(solution)/shard_map/ppermute | solution.py:256
  106.8 2.4 %reverse_bitcast_fusion = bf16[3,3,256,256]{2,3,1,0:T(8,128)(2,1)} fusion(bf16[3,3,256,256]{3,2,1,0:T(8,128)(2,1)} %param.5), kind=kLoop, calls=%fused_computation.1 | loop fusion | bytes 2359296 | tf_op jit(solution)/shard_map/transpose | solution.py:264
  109.1 2.4 %copy.9 = bf16[3,3,256,256]{3,2,1,0:T(8,128)(2,1)} copy(bf16[3,3,256,256]{2,3,1,0:T(8,128)(2,1)} %reverse_bitcast_fusion) | data formatting | bytes 2359296 | tf_op jit(solution)/shard_map/transpose | solution.py:264
  111.5 0.0 copy-done.1
  111.5 0.0 collective-permute-done.6.near_ref
  111.5 22.1 %backward.1 = (bf16[4096,256]{1,0:T(8,128)(2,1)}, f32[3072,256]{1,0:T(8,128)}) custom-call(bf16[4096,256]{1,0:T(8,128)(2,1)} %bitcast.14, bf16[4096,256]{1,0:T(8,128)(2,1)} %bitcast.5.cot_ref, bf16[4096,256]{1,0:T(8,128)(2,1)} %collective-permute-done.6.near_ref, bf16[2048,256]{1,0:T(8,128)(2,1)} %collective-permute-done.far_lo_ref, ...), custom_call_target="tpu_custom_call" | custom-call | flops 12884901888 | bytes 18874368 | tf_op jit(solution)/shard_map/backward/pallas_call | solution.py:303
  133.6 54.6 %reduce_all.1 = bf16[3072,256]{1,0:T(8,128)(2,1)S(1)} custom-call(f32[3072,256]{1,0:T(8,128)} %get-tuple-element.21.grads_ref), custom_call_target="tpu_custom_call" | custom-call | tf_op jit(solution)/shard_map/reduce_all/pallas_call | solution.py:222
  188.2 0.3 convert_multiply_fusion
  188.5 0.9 slice.25
  189.4 1.6 slice.24
  191.0 0.0 collective-permute-done.5.act2_ref
  191.0 0.0 collective-permute-done.4.act1_ref
  191.0 0.9 copy-done
  191.9 5.6 %temporal.1 = bf16[4096,256]{1,0:T(8,128)(2,1)} custom-call(bf16[4096,256]{1,0:T(8,128)(2,1)S(1)} %bitcast.15, bf16[4096,256]{1,0:T(8,128)(2,1)} %copy-done.1, bf16[4096,256]{1,0:T(8,128)(2,1)} %collective-permute-done.4.act1_ref, bf16[4096,256]{1,0:T(8,128)(2,1)} %collective-permute-done.5.act2_ref, bf16[3,256,256]{2,1,0:T(8,128)(2,1)S(1)} %copy-done.2), custom_call_target="tpu_custom_call" | custom-call | flops 1610612736 | bytes 10485760 | tf_op jit(solution)/shard_map/temporal/pallas_call | solution.py:325
  (1 shorter events, 0.0 us)
Async XLA Ops:
  0.6 5.8 %copy-start.3 = (bf16[3,3,256,256]{3,2,1,0:T(8,128)(2,1)S(1)}, bf16[3,3,256,256]{3,2,1,0:T(8,128)(2,1)}, u32[]{:S(2)}) copy-start(bf16[3,3,256,256]{3,2,1,0:T(8,128)(2,1)} %param.5) | copy-start | bytes 3538948
  2.5 28.4 %collective-permute-start.2 = (bf16[2048,256]{1,0:T(8,128)(2,1)S(1)}, bf16[2048,256]{1,0:T(8,128)(2,1)}, u32[]{:S(2)}, u32[]{:S(2)}) collective-permute-start(bf16[2048,256]{1,0:T(8,128)(2,1)S(1)} %bitcast.22), channel_id=1, source_target_pairs={{2,0},{3,1},{6,4},{7,5},{10,8},{11,9},{14,12},{15,13},{18,16},{19,... | collective-permute-start | bytes 3145736 | tf_op jit(solution)/shard_map/ppermute | solution.py:256
  3.8 48.7 %collective-permute-start = (bf16[2048,256]{1,0:T(8,128)(2,1)S(1)}, bf16[2048,256]{1,0:T(8,128)(2,1)}, u32[]{:S(2)}, u32[]{:S(2)}) collective-permute-start(bf16[2048,256]{1,0:T(8,128)(2,1)S(1)} %bitcast.21), channel_id=1, source_target_pairs={{2,0},{3,1},{6,4},{7,5},{10,8},{11,9},{14,12},{15,13},{18,16},{19,... | collective-permute-start | bytes 3145736 | tf_op jit(solution)/shard_map/ppermute | solution.py:256
  5.1 106.4 %collective-permute-start.6 = (bf16[4096,256]{1,0:T(8,128)(2,1)}, bf16[4096,256]{1,0:T(8,128)(2,1)}, u32[]{:S(2)}, u32[]{:S(2)}) collective-permute-start(bf16[4096,256]{1,0:T(8,128)(2,1)} %bitcast.5.cot_ref), channel_id=1, source_target_pairs={{1,0},{3,2},{5,4},{7,6},{9,8},{11,10},{13,12},{15,14},{17,16},{19,... | collective-permute-start | bytes 6291464 | tf_op jit(solution)/shard_map/ppermute | solution.py:256
  6.4 56.3 %copy-start.2 = (bf16[3,256,256]{2,1,0:T(8,128)(2,1)S(1)}, bf16[3,256,256]{2,1,0:T(8,128)(2,1)}, u32[]{:S(2)}) copy-start(bf16[3,256,256]{2,1,0:T(8,128)(2,1)} %w_ref.1) | copy-start | bytes 1179652
  15.9 95.6 %copy-start.1 = (bf16[4096,256]{1,0:T(8,128)(2,1)}, bf16[4096,256]{1,0:T(8,128)(2,1)S(1)}, u32[]{:S(2)}) copy-start(bf16[4096,256]{1,0:T(8,128)(2,1)S(1)} %get-tuple-element.16.act_ref) | copy-start | bytes 6291460
  52.6 28.1 %collective-permute-start.1 = (bf16[2048,256]{1,0:T(8,128)(2,1)}, bf16[2048,256]{1,0:T(8,128)(2,1)}, u32[]{:S(2)}, u32[]{:S(2)}) collective-permute-start(bf16[2048,256]{1,0:T(8,128)(2,1)} %collective-permute-done.far_lo_ref), channel_id=1, source_target_pairs={{0,1},{4,5},{8,9},{12,13},{16,17},{20,21},{24,25},{28,29}} | collective-permute-start | bytes 3145736 | tf_op jit(solution)/shard_map/ppermute | solution.py:256
  57.8 43.3 %collective-permute-start.3 = (bf16[2048,256]{1,0:T(8,128)(2,1)}, bf16[2048,256]{1,0:T(8,128)(2,1)}, u32[]{:S(2)}, u32[]{:S(2)}) collective-permute-start(bf16[2048,256]{1,0:T(8,128)(2,1)} %collective-permute-done.2.far_hi_ref), channel_id=1, source_target_pairs={{0,1},{4,5},{8,9},{12,13},{16,17},{20,21},{24,25},{28,29}} | collective-permute-start | bytes 3145736 | tf_op jit(solution)/shard_map/ppermute | solution.py:256
  60.0 131.0 %collective-permute-start.5 = (bf16[4096,256]{1,0:T(8,128)(2,1)S(1)}, bf16[4096,256]{1,0:T(8,128)(2,1)}, u32[]{:S(2)}, u32[]{:S(2)}) collective-permute-start(bf16[4096,256]{1,0:T(8,128)(2,1)S(1)} %get-tuple-element.16.act_ref), channel_id=1, source_target_pairs={{0,2},{1,3},{4,6},{5,7},{8,10},{9,11},{12,14},{13,15},{16,18},{17,... | collective-permute-start | bytes 6291464 | tf_op jit(solution)/shard_map/ppermute | solution.py:256
  101.1 89.9 %collective-permute-start.4 = (bf16[4096,256]{1,0:T(8,128)(2,1)S(1)}, bf16[4096,256]{1,0:T(8,128)(2,1)}, u32[]{:S(2)}, u32[]{:S(2)}) collective-permute-start(bf16[4096,256]{1,0:T(8,128)(2,1)S(1)} %get-tuple-element.16.act_ref), channel_id=1, source_target_pairs={{0,1},{1,2},{2,3},{4,5},{5,6},{6,7},{8,9},{9,10},{10,11},{12,13},{... | collective-permute-start | bytes 6291464 | tf_op jit(solution)/shard_map/ppermute | solution.py:256
  189.4 2.4 %copy-start = (bf16[64,64,256]{2,1,0:T(8,128)(2,1)S(1)}, bf16[64,64,256]{2,1,0:T(8,128)(2,1)}, u32[]{:S(2)}) copy-start(bf16[64,64,256]{2,1,0:T(8,128)(2,1)} %param.4) | copy-start | bytes 6291460

commit v3 on v2

--- a/solution.py
+++ b/solution.py
@@ -59,7 +59,7 @@
 
 
 def backward_kernel(
-    width, x_ref, cot_ref, near_ref, far_lo_ref, far_hi_ref, via_lo_ref, via_hi_ref, act_ref, slope_ref, wt_ref, wf_ref,
+    width, x_ref, cot_ref, cot1_ref, cot2_ref, act_ref, slope_ref, wt_ref, wf_ref,
     grad_in_ref, grads_ref, g3, temporal, spatial,
 ):
     step = pl.program_id(0)
@@ -75,12 +75,9 @@
     def _():
         act_t = act_ref[...].T
         grad_act = jnp.zeros((cells, channels), F32)
-        low = step < BLOCKS // 2
-        next1 = near_ref[...] + jnp.where(low, via_lo_ref[...], via_hi_ref[...])
-        next2 = jnp.where(low, far_lo_ref[...], far_hi_ref[...])
-        for tap, later in enumerate((cot_ref[...], next1, next2)):
-            grad_act = grad_act + jnp.dot(later, wt_ref[tap], preferred_element_type=F32)
-            temporal[tap] += jnp.dot(act_t, later, preferred_element_type=F32)
+        for tap, ref in enumerate((cot_ref, cot1_ref, cot2_ref)):
+            grad_act = grad_act + jnp.dot(ref[...], wt_ref[tap], preferred_element_type=F32)
+            temporal[tap] += jnp.dot(act_t, ref[...], preferred_element_type=F32)
         grad_pre = grad_act * slope_ref[...]
         store_shifted(g3, pl.multiple_of(width + step * cells, width), grad_pre, width)
 
@@ -247,18 +244,16 @@
         dimension_semantics=("arbitrary",), vmem_limit_bytes=VMEM_LIMIT
     )
 
-    def move(values, *steps):
+    def shift(values, by):
         pairs = [
-            (clip + source, clip + target)
-            for clip in range(0, sp_count, FRAMES)
-            for source, target in steps
+            (i, i + by)
+            for i in range(sp_count)
+            if 0 <= i + by < sp_count and (i + by) // FRAMES == i // FRAMES
         ]
         return lax.ppermute(values, "sp", pairs)
 
-    middle = cells // 2
-    far_lo = move(cot[:middle], (2, 0), (3, 1))
-    near = move(cot, (1, 0), (3, 2))
-    far_hi = move(cot[middle:], (2, 0), (3, 1))
+    cot1 = shift(cot, -1)
+    cot2 = shift(cot, -2)
 
     w3 = spatial_weight.reshape(3, 3 * channels, channels)
     wf = spatial_weight[::-1, ::-1].transpose(0, 1, 3, 2).reshape(3, 3 * channels, channels)
@@ -283,28 +278,18 @@
         name="forward",
     )(x, w3)
 
-    act2 = move(act, (0, 2), (1, 3))
-    far_lo, _ = lax.optimization_barrier((far_lo, act))
-    via_lo = move(far_lo, (0, 1))
-    far_hi, _ = lax.optimization_barrier((far_hi, act))
-    via_hi = move(far_hi, (0, 1))
-    act_late, via_lo, via_hi = lax.optimization_barrier((act, via_lo, via_hi))
-    act1 = move(act_late, (0, 1), (1, 2), (2, 3))
+    act1 = shift(act, 1)
+    act2 = shift(act, 2)
 
     first = pl.BlockSpec((block, channels), lambda step: (jnp.minimum(step, BLOCKS - 1), 0))
     second = pl.BlockSpec((block, channels), lambda step: (jnp.maximum(step - BLOCKS, 0), 0))
     both = pl.BlockSpec((block, channels), lambda step: (step % BLOCKS, 0))
-    lo = pl.BlockSpec((block, channels), lambda step: (jnp.minimum(step, BLOCKS // 2 - 1), 0))
-    hi = pl.BlockSpec(
-        (block, channels),
-        lambda step: (jnp.clip(step - BLOCKS // 2, 0, BLOCKS // 2 - 1), 0),
-    )
     grads_shape = jax.ShapeDtypeStruct((12 * channels, channels), F32)
     grad_in, grads = pl.pallas_call(
         functools.partial(backward_kernel, width),
         grid=(2 * BLOCKS,),
         out_shape=(frame, grads_shape),
-        in_specs=[second, both, first, lo, hi, lo, hi, first, first, whole(wt), whole(wf)],
+        in_specs=[second, both, first, first, first, first, whole(wt), whole(wf)],
         out_specs=(second, whole(grads_shape)),
         scratch_shapes=[
             padded,
@@ -318,7 +303,7 @@
             transcendentals=0,
         ),
         name="backward",
-    )(x, cot, near, far_lo, far_hi, via_lo, via_hi, act, slope, wt, wf)
+    )(x, cot, cot1, cot2, act, slope, wt, wf)
 
     reduced = reduce_all(grads)
 

time: 198 us -> 175 us (0.88)
  waiting for transfers between devices: 74.8 us -> 18.7 us
  Pallas kernels: 91.8 us -> 127 us
  starting transfers between devices: 19.8 us -> 17.4 us
    ppermute x7 -> x4, waiting for transfers between devices: 74.8 us -> 18.7 us  [shift(): return lax.ppermute(values, 'sp', pairs)]
    pallas_call x1, Pallas kernels: 54.6 us -> 92 us  [reduce_all(): pl.pallas_call(functools.partial(reduce_kernel, bits, chunks), out_shape=...]
    ppermute x7 -> x4, starting transfers between devices: 19.8 us -> 17.4 us  [shift(): return lax.ppermute(values, 'sp', pairs)]
    pallas_call x1, Pallas kernels: 22.1 us -> 20 us  [local(): pl.pallas_call(functools.partial(backward_kernel, width), grid=(2 * BLOCK...]
  transfers between devices with their start and end apart: 7 -> 4, of which waited for: 4 -> 2; matrix products, arithmetic and copies ran while one was open for 4% -> 4% of each run, Pallas kernels for 44% -> 70%
where the time goes in v3:
time: 175 us; the launch traced here: 174 us
  Pallas kernels  127 us (73%)
  waiting for transfers between devices  18.7 us (11%)
  starting transfers between devices  17.4 us (10%)
  local copies, waits for them, and re-layouts  10.1 us (6%)
    pallas_call x1, Pallas kernels, reduce_all(): pl.pallas_call(functools.partial(reduce_kernel, bits, chunks), out_shape=...  92 us
    pallas_call x1, Pallas kernels, local(): pl.pallas_call(functools.partial(backward_kernel, width), grid=(2 * BLOCK...  20 us
    ppermute x4, waiting for transfers between devices, shift(): return lax.ppermute(values, 'sp', pairs)  18.7 us
    ppermute x4, starting transfers between devices, shift(): return lax.ppermute(values, 'sp', pairs)  17.4 us
    pallas_call x1, Pallas kernels, local(): pl.pallas_call(functools.partial(forward_kernel, width), grid=(BLOCKS,),...  9.65 us
    pallas_call x1, Pallas kernels, local(): pl.pallas_call(temporal_kernel, grid=(BLOCKS,), out_shape=frame, in_specs...  5.65 us
    transpose x2, local copies, waits for them, and re-layouts, local(): spatial_weight[::-1, ::-1].transpose(0, 1, 3, 2)  4.88 us
  transfers between devices with their start and end apart: 4, of which 2 were waited for; matrix products, arithmetic and copies ran while one was open for 4% of the time, Pallas kernels for 70%

profile of v3, /device:TPU:0, one launch (start us, length us, event | category | flops | bytes accessed | tf_op | source)
XLA Modules:
  0.0 174.5 jit_solution(9916546874861256089)
XLA Ops:
  0.6 1.3 collective-permute-start.3
  1.9 1.3 collective-permute-start.2
  3.2 0.0 copy-start.2
  3.2 1.3 copy-done.2
  4.5 0.0 copy-start.1
  4.5 9.7 %forward.1 = (bf16[4096,256]{1,0:T(8,128)(2,1)}, f32[4096,256]{1,0:T(8,128)}) custom-call(bf16[4096,256]{1,0:T(8,128)(2,1)} %bitcast.11, bf16[3,768,256]{2,1,0:T(8,128)(2,1)S(1)} %bitcast.14), custom_call_target="tpu_custom_call" | custom-call | flops 4831838208 | bytes 8388608 | tf_op jit(solution)/shard_map/forward/pallas_call | solution.py:265
  14.2 8.4 %collective-permute-start.1 = (bf16[4096,256]{1,0:T(8,128)(2,1)}, bf16[4096,256]{1,0:T(8,128)(2,1)}, u32[]{:S(2)}, u32[]{:S(2)}) collective-permute-start(bf16[4096,256]{1,0:T(8,128)(2,1)} %get-tuple-element.8.act_ref), channel_id=1, source_target_pairs={{0,2},{1,3},{4,6},{5,7},{8,10},{9,11},{12,14},{13,15},{16,18},{17,... | collective-permute-start | bytes 6291464 | tf_op jit(solution)/shard_map/ppermute | solution.py:253
  22.5 6.4 %collective-permute-start = (bf16[4096,256]{1,0:T(8,128)(2,1)}, bf16[4096,256]{1,0:T(8,128)(2,1)}, u32[]{:S(2)}, u32[]{:S(2)}) collective-permute-start(bf16[4096,256]{1,0:T(8,128)(2,1)} %get-tuple-element.8.act_ref), channel_id=1, source_target_pairs={{0,1},{1,2},{2,3},{4,5},{5,6},{6,7},{8,9},{9,10},{10,11},{12,13},{... | collective-permute-start | bytes 6291464 | tf_op jit(solution)/shard_map/ppermute | solution.py:253
  28.9 0.0 copy-done.1
  28.9 0.2 copy.8
  29.1 0.0 copy-start
  29.1 2.5 %reverse_bitcast_fusion = bf16[3,3,256,256]{2,3,1,0:T(8,128)(2,1)} fusion(bf16[3,3,256,256]{3,2,1,0:T(8,128)(2,1)} %param.5), kind=kLoop, calls=%fused_computation.1 | loop fusion | bytes 2359296 | tf_op jit(solution)/shard_map/transpose | solution.py:259
  31.6 2.4 %copy.9 = bf16[3,3,256,256]{3,2,1,0:T(8,128)(2,1)} copy(bf16[3,3,256,256]{2,3,1,0:T(8,128)(2,1)} %reverse_bitcast_fusion) | data formatting | bytes 2359296 | tf_op jit(solution)/shard_map/transpose | solution.py:259
  34.0 17.7 %collective-permute-done.3.cot2_ref = bf16[4096,256]{1,0:T(8,128)(2,1)} collective-permute-done((bf16[4096,256]{1,0:T(8,128)(2,1)}, bf16[4096,256]{1,0:T(8,128)(2,1)}, u32[]{:S(2)}, u32[]{:S(2)}) %collective-permute-start.3) | collective-permute-done | bytes 2097184 | tf_op jit(solution)/shard_map/ppermute | solution.py:253
  51.7 1.0 collective-permute-done.2.cot1_ref
  52.7 0.0 copy-done
  52.7 0.0 copy-start.3
  52.8 1.3 copy-done.3
  54.0 20.0 %backward.1 = (bf16[4096,256]{1,0:T(8,128)(2,1)}, f32[3072,256]{1,0:T(8,128)}) custom-call(bf16[4096,256]{1,0:T(8,128)(2,1)S(1)} %bitcast.12, bf16[4096,256]{1,0:T(8,128)(2,1)} %bitcast.22, bf16[4096,256]{1,0:T(8,128)(2,1)} %collective-permute-done.2.cot1_ref, bf16[4096,256]{1,0:T(8,128)(2,1)} %collective-permute-done.3.cot2_ref, ...), custom_call_target="tpu_custom_call" | custom-call | flops 12884901888 | bytes 18874368 | tf_op jit(solution)/shard_map/backward/pallas_call | solution.py:288
  74.0 92.0 %reduce_all.1 = bf16[3072,256]{1,0:T(8,128)(2,1)S(1)} custom-call(f32[3072,256]{1,0:T(8,128)} %get-tuple-element.11.grads_ref), custom_call_target="tpu_custom_call" | custom-call | tf_op jit(solution)/shard_map/reduce_all/pallas_call | solution.py:219
  166.0 0.3 convert_multiply_fusion
  166.3 0.9 slice.9
  167.3 1.6 slice.8
  168.8 0.0 collective-permute-done.1.act2_ref
  168.8 0.0 collective-permute-done.act1_ref
  168.8 5.7 %temporal.1 = bf16[4096,256]{1,0:T(8,128)(2,1)} custom-call(bf16[4096,256]{1,0:T(8,128)(2,1)S(1)} %bitcast.13, bf16[4096,256]{1,0:T(8,128)(2,1)} %get-tuple-element.8.act_ref, bf16[4096,256]{1,0:T(8,128)(2,1)} %collective-permute-done.act1_ref, bf16[4096,256]{1,0:T(8,128)(2,1)} %collective-permute-done.1.act2_ref, bf16[3,256,256]{2,1,0:T(8,128)(2,1)S(1)} %copy-done.1), custom_call_target="tpu_custom_call" | custom-call | flops 1610612736 | bytes 10485760 | tf_op jit(solution)/shard_map/temporal/pallas_call | solution.py:310
Async XLA Ops:
  0.6 51.1 %collective-permute-start.3 = (bf16[4096,256]{1,0:T(8,128)(2,1)}, bf16[4096,256]{1,0:T(8,128)(2,1)}, u32[]{:S(2)}, u32[]{:S(2)}) collective-permute-start(bf16[4096,256]{1,0:T(8,128)(2,1)} %bitcast.20), channel_id=1, source_target_pairs={{2,0},{3,1},{6,4},{7,5},{10,8},{11,9},{14,12},{15,13},{18,16},{19,... | collective-permute-start | bytes 6291464 | tf_op jit(solution)/shard_map/ppermute | solution.py:253
  1.9 50.8 %collective-permute-start.2 = (bf16[4096,256]{1,0:T(8,128)(2,1)}, bf16[4096,256]{1,0:T(8,128)(2,1)}, u32[]{:S(2)}, u32[]{:S(2)}) collective-permute-start(bf16[4096,256]{1,0:T(8,128)(2,1)} %bitcast.21), channel_id=1, source_target_pairs={{1,0},{2,1},{3,2},{5,4},{6,5},{7,6},{9,8},{10,9},{11,10},{13,12},{... | collective-permute-start | bytes 6291464 | tf_op jit(solution)/shard_map/ppermute | solution.py:253
  3.2 1.3 copy-start.2
  4.5 24.4 %copy-start.1 = (bf16[3,256,256]{2,1,0:T(8,128)(2,1)S(1)}, bf16[3,256,256]{2,1,0:T(8,128)(2,1)}, u32[]{:S(2)}) copy-start(bf16[3,256,256]{2,1,0:T(8,128)(2,1)} %w_ref.1) | copy-start | bytes 1179652
  14.2 154.7 %collective-permute-start.1 = (bf16[4096,256]{1,0:T(8,128)(2,1)}, bf16[4096,256]{1,0:T(8,128)(2,1)}, u32[]{:S(2)}, u32[]{:S(2)}) collective-permute-start(bf16[4096,256]{1,0:T(8,128)(2,1)} %get-tuple-element.8.act_ref), channel_id=1, source_target_pairs={{0,2},{1,3},{4,6},{5,7},{8,10},{9,11},{12,14},{13,15},{16,18},{17,... | collective-permute-start | bytes 6291464 | tf_op jit(solution)/shard_map/ppermute | solution.py:253
  22.5 146.3 %collective-permute-start = (bf16[4096,256]{1,0:T(8,128)(2,1)}, bf16[4096,256]{1,0:T(8,128)(2,1)}, u32[]{:S(2)}, u32[]{:S(2)}) collective-permute-start(bf16[4096,256]{1,0:T(8,128)(2,1)} %get-tuple-element.8.act_ref), channel_id=1, source_target_pairs={{0,1},{1,2},{2,3},{4,5},{5,6},{6,7},{8,9},{9,10},{10,11},{12,13},{... | collective-permute-start | bytes 6291464 | tf_op jit(solution)/shard_map/ppermute | solution.py:253
  29.1 23.6 %copy-start = (bf16[64,64,256]{2,1,0:T(8,128)(2,1)S(1)}, bf16[64,64,256]{2,1,0:T(8,128)(2,1)}, u32[]{:S(2)}) copy-start(bf16[64,64,256]{2,1,0:T(8,128)(2,1)} %param.4) | copy-start | bytes 6291460
  52.7 1.3 copy-start.3

commit v4 on v2

--- a/solution.py
+++ b/solution.py
@@ -258,7 +258,6 @@
     middle = cells // 2
     far_lo = move(cot[:middle], (2, 0), (3, 1))
     near = move(cot, (1, 0), (3, 2))
-    far_hi = move(cot[middle:], (2, 0), (3, 1))
 
     w3 = spatial_weight.reshape(3, 3 * channels, channels)
     wf = spatial_weight[::-1, ::-1].transpose(0, 1, 3, 2).reshape(3, 3 * channels, channels)
@@ -283,10 +282,10 @@
         name="forward",
     )(x, w3)
 
+    far_lo, act = lax.optimization_barrier((far_lo, act))
+    via_lo = move(far_lo, (0, 1))
+    far_hi = move(lax.optimization_barrier((cot[middle:], far_lo))[0], (2, 0), (3, 1))
     act2 = move(act, (0, 2), (1, 3))
-    far_lo, _ = lax.optimization_barrier((far_lo, act))
-    via_lo = move(far_lo, (0, 1))
-    far_hi, _ = lax.optimization_barrier((far_hi, act))
     via_hi = move(far_hi, (0, 1))
     act_late, via_lo, via_hi = lax.optimization_barrier((act, via_lo, via_hi))
     act1 = move(act_late, (0, 1), (1, 2), (2, 3))

time: 198 us -> 199 us (level)
  waiting for transfers between devices: 74.8 us -> 52.4 us
  Pallas kernels: 91.8 us -> 111 us
  starting transfers between devices: 19.8 us -> 24 us
    ppermute x7, waiting for transfers between devices: 74.8 us -> 52.4 us  [move(): return lax.ppermute(values, 'sp', pairs)]
    pallas_call x1, Pallas kernels: 54.6 us -> 73.7 us  [reduce_all(): pl.pallas_call(functools.partial(reduce_kernel, bits, chunks), out_shape=...]
    ppermute x7, starting transfers between devices: 19.8 us -> 24 us  [move(): return lax.ppermute(values, 'sp', pairs)]
  transfers between devices with their start and end apart: 7 -> 7, of which waited for: 4 -> 3; matrix products, arithmetic and copies ran while one was open for 4% -> 4% of each run, Pallas kernels for 44% -> 53%
where the time goes in v4:
time: 199 us; the launch traced here: 198 us
  Pallas kernels  111 us (56%)
  waiting for transfers between devices  52.4 us (26%)
  starting transfers between devices  24 us (12%)
  local copies, waits for them, and re-layouts  10.2 us (5%)
    pallas_call x1, Pallas kernels, reduce_all(): pl.pallas_call(functools.partial(reduce_kernel, bits, chunks), out_shape=...  73.7 us
    ppermute x7, waiting for transfers between devices, move(): return lax.ppermute(values, 'sp', pairs)  52.4 us
    ppermute x7, starting transfers between devices, move(): return lax.ppermute(values, 'sp', pairs)  24 us
    pallas_call x1, Pallas kernels, local(): pl.pallas_call(functools.partial(backward_kernel, width), grid=(2 * BLOCK...  22.1 us
    pallas_call x1, Pallas kernels, local(): pl.pallas_call(functools.partial(forward_kernel, width), grid=(BLOCKS,),...  9.44 us
    pallas_call x1, Pallas kernels, local(): pl.pallas_call(temporal_kernel, grid=(BLOCKS,), out_shape=frame, in_specs...  5.65 us
    transpose x2, local copies, waits for them, and re-layouts, local(): spatial_weight[::-1, ::-1].transpose(0, 1, 3, 2)  4.73 us
  transfers between devices with their start and end apart: 7, of which 3 were waited for; matrix products, arithmetic and copies ran while one was open for 4% of the time, Pallas kernels for 53%

profile of v4, /device:TPU:0, one launch (start us, length us, event | category | flops | bytes accessed | tf_op | source)
XLA Modules:
  0.0 198.4 jit_solution(3170372919823862133)
XLA Ops:
  0.6 0.0 copy-start.3
  0.6 1.9 fusion
  2.5 1.3 collective-permute-start
  3.8 0.0 copy-done.3
  3.8 0.0 copy-start.2
  3.8 9.4 %forward.1 = (bf16[4096,256]{1,0:T(8,128)(2,1)S(1)}, f32[4096,256]{1,0:T(8,128)}) custom-call(bf16[4096,256]{1,0:T(8,128)(2,1)} %bitcast.13, bf16[3,768,256]{2,1,0:T(8,128)(2,1)S(1)} %bitcast.16), custom_call_target="tpu_custom_call" | custom-call | flops 4831838208 | bytes 8388608 | tf_op jit(solution)/shard_map/forward/pallas_call | solution.py:269
  13.3 16.8 %collective-permute-done.far_lo_ref = bf16[2048,256]{1,0:T(8,128)(2,1)} collective-permute-done((bf16[2048,256]{1,0:T(8,128)(2,1)S(1)}, bf16[2048,256]{1,0:T(8,128)(2,1)}, u32[]{:S(2)}, u32[]{:S(2)}) %collective-permute-start) | collective-permute-done | bytes 1048608 | tf_op jit(solution)/shard_map/ppermute | solution.py:256
  30.1 1.3 collective-permute-start.2
  31.4 1.3 collective-permute-start.6
  32.7 6.8 %collective-permute-start.1 = (bf16[2048,256]{1,0:T(8,128)(2,1)}, bf16[2048,256]{1,0:T(8,128)(2,1)}, u32[]{:S(2)}, u32[]{:S(2)}) collective-permute-start(bf16[2048,256]{1,0:T(8,128)(2,1)} %collective-permute-done.far_lo_ref), channel_id=1, source_target_pairs={{0,1},{4,5},{8,9},{12,13},{16,17},{20,21},{24,25},{28,29}} | collective-permute-start | bytes 3145736 | tf_op jit(solution)/shard_map/ppermute | solution.py:256
  39.5 16.9 %collective-permute-done.2.far_hi_ref = bf16[2048,256]{1,0:T(8,128)(2,1)} collective-permute-done((bf16[2048,256]{1,0:T(8,128)(2,1)S(1)}, bf16[2048,256]{1,0:T(8,128)(2,1)}, u32[]{:S(2)}, u32[]{:S(2)}) %collective-permute-start.2) | collective-permute-done | bytes 1048608 | tf_op jit(solution)/shard_map/ppermute | solution.py:256
  56.4 4.9 %collective-permute-start.3 = (bf16[2048,256]{1,0:T(8,128)(2,1)}, bf16[2048,256]{1,0:T(8,128)(2,1)}, u32[]{:S(2)}, u32[]{:S(2)}) collective-permute-start(bf16[2048,256]{1,0:T(8,128)(2,1)} %collective-permute-done.2.far_hi_ref), channel_id=1, source_target_pairs={{0,1},{4,5},{8,9},{12,13},{16,17},{20,21},{24,25},{28,29}} | collective-permute-start | bytes 3145736 | tf_op jit(solution)/shard_map/ppermute | solution.py:256
  61.3 0.0 copy-done.2
  61.3 0.2 copy.8
  61.5 2.7 %collective-permute-start.5 = (bf16[4096,256]{1,0:T(8,128)(2,1)S(1)}, bf16[4096,256]{1,0:T(8,128)(2,1)}, u32[]{:S(2)}, u32[]{:S(2)}) collective-permute-start(bf16[4096,256]{1,0:T(8,128)(2,1)S(1)} %get-tuple-element.18.act_ref), channel_id=1, source_target_pairs={{0,2},{1,3},{4,6},{5,7},{8,10},{9,11},{12,14},{13,15},{16,18},{17,... | collective-permute-start | bytes 6291464 | tf_op jit(solution)/shard_map/ppermute | solution.py:256
  64.2 0.0 collective-permute-done.1.via_lo_ref
  64.2 18.7 %collective-permute-done.3.via_hi_ref = bf16[2048,256]{1,0:T(8,128)(2,1)} collective-permute-done((bf16[2048,256]{1,0:T(8,128)(2,1)}, bf16[2048,256]{1,0:T(8,128)(2,1)}, u32[]{:S(2)}, u32[]{:S(2)}) %collective-permute-start.3) | collective-permute-done | bytes 1048608 | tf_op jit(solution)/shard_map/ppermute | solution.py:256
  82.9 5.7 %collective-permute-start.4 = (bf16[4096,256]{1,0:T(8,128)(2,1)S(1)}, bf16[4096,256]{1,0:T(8,128)(2,1)}, u32[]{:S(2)}, u32[]{:S(2)}) collective-permute-start(bf16[4096,256]{1,0:T(8,128)(2,1)S(1)} %get-tuple-element.18.act_ref), channel_id=1, source_target_pairs={{0,1},{1,2},{2,3},{4,5},{5,6},{6,7},{8,9},{9,10},{10,11},{12,13},{... | collective-permute-start | bytes 6291464 | tf_op jit(solution)/shard_map/ppermute | solution.py:256
  88.6 2.4 %reverse_bitcast_fusion = bf16[3,3,256,256]{2,3,1,0:T(8,128)(2,1)} fusion(bf16[3,3,256,256]{3,2,1,0:T(8,128)(2,1)} %param.5), kind=kLoop, calls=%fused_computation.1 | loop fusion | bytes 2359296 | tf_op jit(solution)/shard_map/transpose | solution.py:263
  90.9 2.4 %copy.9 = bf16[3,3,256,256]{3,2,1,0:T(8,128)(2,1)} copy(bf16[3,3,256,256]{2,3,1,0:T(8,128)(2,1)} %reverse_bitcast_fusion) | data formatting | bytes 2359296 | tf_op jit(solution)/shard_map/transpose | solution.py:263
  93.3 0.0 copy-done.1
  93.3 0.0 collective-permute-done.6.near_ref
  93.3 22.1 %backward.1 = (bf16[4096,256]{1,0:T(8,128)(2,1)}, f32[3072,256]{1,0:T(8,128)}) custom-call(bf16[4096,256]{1,0:T(8,128)(2,1)} %bitcast.14, bf16[4096,256]{1,0:T(8,128)(2,1)} %bitcast.5.cot_ref, bf16[4096,256]{1,0:T(8,128)(2,1)} %collective-permute-done.6.near_ref, bf16[2048,256]{1,0:T(8,128)(2,1)} %collective-permute-done.far_lo_ref, ...), custom_call_target="tpu_custom_call" | custom-call | flops 12884901888 | bytes 18874368 | tf_op jit(solution)/shard_map/backward/pallas_call | solution.py:302
  115.4 73.7 %reduce_all.1 = bf16[3072,256]{1,0:T(8,128)(2,1)S(1)} custom-call(f32[3072,256]{1,0:T(8,128)} %get-tuple-element.23.grads_ref), custom_call_target="tpu_custom_call" | custom-call | tf_op jit(solution)/shard_map/reduce_all/pallas_call | solution.py:222
  189.1 0.3 convert_multiply_fusion
  189.4 0.9 slice.25
  190.3 0.0 copy-start
  190.3 1.6 slice.24
  191.9 0.0 collective-permute-done.5.act2_ref
  191.9 0.0 collective-permute-done.4.act1_ref
  191.9 0.9 copy-done
  192.8 5.6 %temporal.1 = bf16[4096,256]{1,0:T(8,128)(2,1)} custom-call(bf16[4096,256]{1,0:T(8,128)(2,1)S(1)} %bitcast.15, bf16[4096,256]{1,0:T(8,128)(2,1)} %copy-done.1, bf16[4096,256]{1,0:T(8,128)(2,1)} %collective-permute-done.4.act1_ref, bf16[4096,256]{1,0:T(8,128)(2,1)} %collective-permute-done.5.act2_ref, bf16[3,256,256]{2,1,0:T(8,128)(2,1)S(1)} %copy-done.2), custom_call_target="tpu_custom_call" | custom-call | flops 1610612736 | bytes 10485760 | tf_op jit(solution)/shard_map/temporal/pallas_call | solution.py:324
  (1 shorter events, 0.0 us)
Async XLA Ops:
  0.6 3.2 %copy-start.3 = (bf16[3,3,256,256]{3,2,1,0:T(8,128)(2,1)S(1)}, bf16[3,3,256,256]{3,2,1,0:T(8,128)(2,1)}, u32[]{:S(2)}) copy-start(bf16[3,3,256,256]{3,2,1,0:T(8,128)(2,1)} %param.5) | copy-start | bytes 3538948
  2.5 27.6 %collective-permute-start = (bf16[2048,256]{1,0:T(8,128)(2,1)S(1)}, bf16[2048,256]{1,0:T(8,128)(2,1)}, u32[]{:S(2)}, u32[]{:S(2)}) collective-permute-start(bf16[2048,256]{1,0:T(8,128)(2,1)S(1)} %bitcast.22), channel_id=1, source_target_pairs={{2,0},{3,1},{6,4},{7,5},{10,8},{11,9},{14,12},{15,13},{18,16},{19,... | collective-permute-start | bytes 3145736 | tf_op jit(solution)/shard_map/ppermute | solution.py:256
  3.8 57.4 %copy-start.2 = (bf16[3,256,256]{2,1,0:T(8,128)(2,1)S(1)}, bf16[3,256,256]{2,1,0:T(8,128)(2,1)}, u32[]{:S(2)}) copy-start(bf16[3,256,256]{2,1,0:T(8,128)(2,1)} %w_ref.1) | copy-start | bytes 1179652
  13.3 80.0 %copy-start.1 = (bf16[4096,256]{1,0:T(8,128)(2,1)}, bf16[4096,256]{1,0:T(8,128)(2,1)S(1)}, u32[]{:S(2)}) copy-start(bf16[4096,256]{1,0:T(8,128)(2,1)S(1)} %get-tuple-element.18.act_ref) | copy-start | bytes 6291460
  30.1 26.3 %collective-permute-start.2 = (bf16[2048,256]{1,0:T(8,128)(2,1)S(1)}, bf16[2048,256]{1,0:T(8,128)(2,1)}, u32[]{:S(2)}, u32[]{:S(2)}) collective-permute-start(bf16[2048,256]{1,0:T(8,128)(2,1)S(1)} %bitcast.21), channel_id=1, source_target_pairs={{2,0},{3,1},{6,4},{7,5},{10,8},{11,9},{14,12},{15,13},{18,16},{19,... | collective-permute-start | bytes 3145736 | tf_op jit(solution)/shard_map/ppermute | solution.py:256
  31.4 61.9 %collective-permute-start.6 = (bf16[4096,256]{1,0:T(8,128)(2,1)}, bf16[4096,256]{1,0:T(8,128)(2,1)}, u32[]{:S(2)}, u32[]{:S(2)}) collective-permute-start(bf16[4096,256]{1,0:T(8,128)(2,1)} %bitcast.5.cot_ref), channel_id=1, source_target_pairs={{1,0},{3,2},{5,4},{7,6},{9,8},{11,10},{13,12},{15,14},{17,16},{19,... | collective-permute-start | bytes 6291464 | tf_op jit(solution)/shard_map/ppermute | solution.py:256
  32.7 31.5 %collective-permute-start.1 = (bf16[2048,256]{1,0:T(8,128)(2,1)}, bf16[2048,256]{1,0:T(8,128)(2,1)}, u32[]{:S(2)}, u32[]{:S(2)}) collective-permute-start(bf16[2048,256]{1,0:T(8,128)(2,1)} %collective-permute-done.far_lo_ref), channel_id=1, source_target_pairs={{0,1},{4,5},{8,9},{12,13},{16,17},{20,21},{24,25},{28,29}} | collective-permute-start | bytes 3145736 | tf_op jit(solution)/shard_map/ppermute | solution.py:256
  56.4 26.4 %collective-permute-start.3 = (bf16[2048,256]{1,0:T(8,128)(2,1)}, bf16[2048,256]{1,0:T(8,128)(2,1)}, u32[]{:S(2)}, u32[]{:S(2)}) collective-permute-start(bf16[2048,256]{1,0:T(8,128)(2,1)} %collective-permute-done.2.far_hi_ref), channel_id=1, source_target_pairs={{0,1},{4,5},{8,9},{12,13},{16,17},{20,21},{24,25},{28,29}} | collective-permute-start | bytes 3145736 | tf_op jit(solution)/shard_map/ppermute | solution.py:256
  61.5 130.4 %collective-permute-start.5 = (bf16[4096,256]{1,0:T(8,128)(2,1)S(1)}, bf16[4096,256]{1,0:T(8,128)(2,1)}, u32[]{:S(2)}, u32[]{:S(2)}) collective-permute-start(bf16[4096,256]{1,0:T(8,128)(2,1)S(1)} %get-tuple-element.18.act_ref), channel_id=1, source_target_pairs={{0,2},{1,3},{4,6},{5,7},{8,10},{9,11},{12,14},{13,15},{16,18},{17,... | collective-permute-start | bytes 6291464 | tf_op jit(solution)/shard_map/ppermute | solution.py:256
  82.9 109.0 %collective-permute-start.4 = (bf16[4096,256]{1,0:T(8,128)(2,1)S(1)}, bf16[4096,256]{1,0:T(8,128)(2,1)}, u32[]{:S(2)}, u32[]{:S(2)}) collective-permute-start(bf16[4096,256]{1,0:T(8,128)(2,1)S(1)} %get-tuple-element.18.act_ref), channel_id=1, source_target_pairs={{0,1},{1,2},{2,3},{4,5},{5,6},{6,7},{8,9},{9,10},{10,11},{12,13},{... | collective-permute-start | bytes 6291464 | tf_op jit(solution)/shard_map/ppermute | solution.py:256
  190.3 2.4 %copy-start = (bf16[64,64,256]{2,1,0:T(8,128)(2,1)S(1)}, bf16[64,64,256]{2,1,0:T(8,128)(2,1)}, u32[]{:S(2)}) copy-start(bf16[64,64,256]{2,1,0:T(8,128)(2,1)} %param.4) | copy-start | bytes 6291460
